TPU v7x, 256 devices: a whole 4x4x8 slice. The times are simulated.
256 devices in a mesh: gx: 32 (over y_hi, z, core), gy: 8 (over x, y_lo).
Axes of the slice: x: 4, y: 4 (y_hi: 2, y_lo: 2; y = y_hi * 2 + y_lo), z: 8, core: 2. Of those that a mesh axis runs over, the one named last changes fastest.
Arguments:
- pressure_head: float32 [32, 128, 1024], P('gx', None, 'gy'), may hold values from -0.8 to -0.1
- material_zone: int32 [32, 128, 1024], P('gx', None, 'gy'), may hold values from 0 to 3
- emitters: int32 [32, 1024], P('gx', 'gy'), may hold values 0 or 1
- oxygen: float32 [32, 128, 1024], P('gx', None, 'gy'), may hold values from 0.05 to 1
- sulfide_rate: float32 [32, 128, 1024], P('gx', None, 'gy'), may hold values from 0.05 to 0.5
- air_flux: float32 [32, 1024], P('gx', 'gy'), may hold values from 0.02 to 0.3
Outputs:
- head_out: float32 [32, 128, 1024], P('gx', None, 'gy')
- oxygen_out: float32 [32, 128, 1024], P('gx', 'gy')
Inputs may be any that keep to these rules, and one draw needn't show every extreme that they name: `material_zone`: material zones index the four parameter sets.
All inputs are finite; a program needn't handle non-finite values. No bound on the sum of `emitters` on one device may be relied on, other than what follows from the above.
Results may differ from a plain program's by a relative error of at most 0.0003.
Values sent between devices are 32-bit elements; how exact they have to be, the bound alone decides.
A program may use at most 64 MiB of HBM per device.

v0:
```python
import jax
import jax.numpy as jnp
from jax import lax
from jax.sharding import PartitionSpec as P

PICARD = 2
SWEEPS = 8
GAS_STEPS = 2


TABLE = (
    (4.0, 2.5, 1.2, 0.8),
    (2.4, 1.9, 1.6, 1.4),
    (0.05, 0.08, 0.1, 0.12),
    (0.38, 0.42, 0.45, 0.4),
    (5.0, 2.0, 0.6, 0.2),
)
flow_step = 2.0
storage_term = 0.01
cond_floor = 0.001
irrigation = 0.3
gas_step = 0.25


def extended(cells, sides, width):
    for axis, dim in sides:
        count = lax.axis_size(axis)
        ends = count - 1
        head = lax.slice_in_dim(cells, 0, width, axis=dim)
        tail = lax.slice_in_dim(cells, cells.shape[dim] - width, cells.shape[dim], axis=dim)
        cells = jnp.concatenate(
            [
                lax.ppermute(tail, axis, [(i, (i + 1) % count) for i in range(ends)]),
                cells,
                lax.ppermute(head, axis, [((i + 1) % count, i) for i in range(ends)]),
            ],
            axis=dim,
        )
    return cells


def zone_params(material_zone):
    result = []
    for entries in TABLE:
        selected = jnp.zeros(material_zone.shape, jnp.float32)
        for number in range(4):
            selected = selected + jnp.where(
                material_zone == number, jnp.float32(entries[number]), jnp.float32(0.0)
            )
        result.append(selected)
    return result


def retention(head_field, params):
    entry_scale, pore_index, residual_water, saturated_water, saturated_cond = params
    suction = jnp.maximum(-head_field, 0.0)
    exponent = 1.0 - 1.0 / pore_index
    scaled = entry_scale * suction
    powered = scaled**pore_index
    effective = (1.0 + powered) ** (-exponent)
    water_content = residual_water + (saturated_water - residual_water) * effective
    capacity = (
        saturated_water - residual_water
    ) * entry_scale * pore_index * exponent * scaled ** (pore_index - 1.0) * (1.0 + powered) ** (
        -exponent - 1.0
    ) + storage_term
    mualem_term = 1.0 - (1.0 - effective ** (1.0 / exponent)) ** exponent
    conductivity = saturated_cond * (jnp.sqrt(effective) * mualem_term * mualem_term + cond_floor)
    return (water_content, capacity, conductivity, effective)


def harmonic(first, second):
    return 2.0 * first * second / (first + second)


def shift_down(values, stride, filler):
    edge = jnp.full((values.shape[0], stride, values.shape[2]), filler, values.dtype)
    return jnp.concatenate([edge, values[:, :-stride]], axis=1)


def shift_up(values, stride, filler):
    edge = jnp.full((values.shape[0], stride, values.shape[2]), filler, values.dtype)
    return jnp.concatenate([values[:, stride:], edge], axis=1)


def neighbours(padded):
    return (padded[:-2, :, 1:-1], padded[2:, :, 1:-1], padded[1:-1, :, :-2], padded[1:-1, :, 2:])


def factor(below_diag, main_diag, above_diag):
    factors = []
    stride = 1
    depth = main_diag.shape[1]
    for levels in range((depth - 1).bit_length()):
        left_mult = -below_diag / shift_down(main_diag, stride, 1.0)
        right_mult = -above_diag / shift_up(main_diag, stride, 1.0)
        new_below = left_mult * shift_down(below_diag, stride, 0.0)
        new_above = right_mult * shift_up(above_diag, stride, 0.0)
        main_diag = (
            main_diag
            + left_mult * shift_down(above_diag, stride, 0.0)
            + right_mult * shift_up(below_diag, stride, 0.0)
        )
        below_diag = new_below
        above_diag = new_above
        factors.append((left_mult, right_mult, stride))
        stride = stride * 2
    return (factors, 1.0 / main_diag)


def apply_factors(factors, inverse, source):
    for left_mult, right_mult, stride in factors:
        source = (
            source
            + left_mult * shift_down(source, stride, 0.0)
            + right_mult * shift_up(source, stride, 0.0)
        )
    return source * inverse


def gas_update(
    conc_full, diff_full, oxygen_now, diffusivity, reaction, storage, upward, top_rows, bottom
):
    sides = [
        (slice(None, -2), slice(1, -1), slice(1, -1)),
        (slice(2, None), slice(1, -1), slice(1, -1)),
        (slice(1, -1), slice(None, -2), slice(1, -1)),
        (slice(1, -1), slice(2, None), slice(1, -1)),
        (slice(1, -1), slice(1, -1), slice(None, -2)),
        (slice(1, -1), slice(1, -1), slice(2, None)),
    ]
    diffusive = jnp.zeros_like(oxygen_now)
    for window in sides:
        diffusive = diffusive + jnp.sqrt(diffusivity * diff_full[window]) * (
            conc_full[window] - oxygen_now
        )
    below_cell = conc_full[1:-1, 2:, 1:-1] + bottom
    change = (
        diffusive
        + 2.0 * diffusivity * (1.0 - oxygen_now) * top_rows
        + upward * (below_cell - oxygen_now)
        - reaction * oxygen_now
    )
    return oxygen_now + storage * change


def sweep_halo(iterate):
    return extended(iterate, (("gx", 0), ("gy", 2)), 1)


def local(pressure_head, material_zone, emitters, oxygen, sulfide_rate, air_flux):
    params = zone_params(material_zone)
    theta_old = retention(pressure_head, params)[0]
    depth = pressure_head.shape[1]
    layer_index = lax.broadcasted_iota(jnp.int32, pressure_head.shape, 1)
    top_rows = (layer_index == 0).astype(jnp.float32)
    bottom = (layer_index == depth - 1).astype(jnp.float32)
    irrigated = top_rows * irrigation * emitters[:, None, :].astype(jnp.float32)
    current = pressure_head
    for picard_pass in range(PICARD):
        theta_now, capacity, conductivity, effective = retention(current, params)
        cond_pad, iterate_pad = (
            extended(conductivity, (("gx", 0), ("gy", 2)), 1),
            extended(current, (("gx", 0), ("gy", 2)), 1),
        )
        lateral = [harmonic(conductivity, other) for other in neighbours(cond_pad)]
        upper_face = harmonic(conductivity, shift_down(conductivity, 1, 0.0))
        lower_face = harmonic(conductivity, shift_up(conductivity, 1, 0.0))
        diagonal = (
            capacity / flow_step
            + lateral[0]
            + lateral[1]
            + lateral[2]
            + lateral[3]
            + upper_face
            + lower_face
        )
        base_source = (
            capacity / flow_step * current
            - (theta_now - theta_old) / flow_step
            + upper_face
            - lower_face
            - bottom * conductivity
            + irrigated
        )
        factors, inverse = factor(-upper_face, diagonal, -lower_face)
        iterate = current
        for sweep_pass in range(SWEEPS):
            if sweep_pass > 0:
                iterate_pad = sweep_halo(iterate)
            beside_all = neighbours(iterate_pad)
            source = (
                base_source
                + lateral[0] * beside_all[0]
                + lateral[1] * beside_all[1]
                + lateral[2] * beside_all[2]
                + lateral[3] * beside_all[3]
            )
            iterate = apply_factors(factors, inverse, source)
        current = iterate
    theta_end, capacity, conductivity, effective = retention(current, params)
    gas_filled = (params[3] - params[2]) * (1.0 - effective)
    diffusivity = gas_filled ** (10.0 / 3.0) / (params[3] * params[3])
    reaction = sulfide_rate * theta_end / params[3]
    storage = gas_step / params[3]
    upward = jnp.broadcast_to(air_flux[:, None, :], current.shape)
    oxygen_now, brick_diffusion, brick_reaction, brick_storage, brick_upward = (
        lax.all_to_all(oxygen, "gy", split_axis=1, concat_axis=2, tiled=True),
        lax.all_to_all(diffusivity, "gy", split_axis=1, concat_axis=2, tiled=True),
        lax.all_to_all(reaction, "gy", split_axis=1, concat_axis=2, tiled=True),
        lax.all_to_all(storage, "gy", split_axis=1, concat_axis=2, tiled=True),
        lax.all_to_all(upward, "gy", split_axis=1, concat_axis=2, tiled=True),
    )
    layers = oxygen_now.shape[1]
    global_layer = lax.axis_index("gy") * layers + lax.broadcasted_iota(
        jnp.int32, oxygen_now.shape, 1
    )
    brick_top = (global_layer == 0).astype(jnp.float32)
    brick_bottom = (global_layer == layers * lax.axis_size("gy") - 1).astype(jnp.float32)
    local_pad = ((0, 0), (0, 0), (1, 1))
    for gas_pass in range(GAS_STEPS):
        if gas_pass == 0:
            conc_rim, diff_rim = (
                extended(oxygen_now, (("gx", 0), ("gy", 1)), 1),
                extended(brick_diffusion, (("gx", 0), ("gy", 1)), 1),
            )
            diff_full = jnp.pad(diff_rim, local_pad)
        else:
            conc_rim = extended(oxygen_now, (("gx", 0), ("gy", 1)), 1)
        oxygen_now = gas_update(
            jnp.pad(conc_rim, local_pad),
            diff_full,
            oxygen_now,
            brick_diffusion,
            brick_reaction,
            brick_storage,
            brick_upward,
            brick_top,
            brick_bottom,
        )
    return (current, oxygen_now)


def solution(mesh):
    return jax.shard_map(
        local,
        mesh=mesh,
        in_specs=(
            P("gx", None, "gy"),
            P("gx", None, "gy"),
            P("gx", "gy"),
            P("gx", None, "gy"),
            P("gx", None, "gy"),
            P("gx", "gy"),
        ),
        out_specs=(P("gx", None, "gy"), P("gx", "gy", None)),
        check_vma=False,
    )
```

profile of v0, /device:TPU:22, one launch (start us, length us, event | category | flops | bytes accessed | tf_op | source)
XLA Modules:
  0.0 584.5 jit_solution(9903271812192870867)
XLA Ops:
  0.6 7.0 %collective-permute-start.3 = (f32[1,128,128]{2,0,1:T(1,128)}, f32[1,128,128]{2,0,1:T(1,128)S(1)}, u32[]{:S(2)}, u32[]{:S(2)}) collective-permute-start(f32[1,128,128]{2,0,1:T(1,128)} %bitcast.314), channel_id=1, source_target_pairs={{8,0},{16,8},{24,16},{32,24},{40,32},{48,40},{56,48},{64,56},{72,6... | collective-permute-start | bytes 196616 | tf_op jit(solution)/shard_map/ppermute | solution.py:35
  9.5 5.6 fusion.4
  17.2 7.3 %collective-permute-start.2 = (f32[1,128,128]{2,0,1:T(1,128)S(1)}, f32[1,128,128]{2,0,1:T(1,128)S(1)}, u32[]{:S(2)}, u32[]{:S(2)}) collective-permute-start(f32[1,128,128]{2,0,1:T(1,128)S(1)} %get-tuple-element.104), channel_id=1, source_target_pairs={{8,0},{16,8},{24,16},{32,24},{40,32},{48,40},{56,48},{64,56},{72,6... | collective-permute-start | bytes 196616 | tf_op jit(solution)/shard_map/ppermute | solution.py:35
  39.3 6.1 %collective-permute-done.7 = f32[3,128,1]{2,0,1:T(4,128)S(1)} collective-permute-done((f32[3,128,1]{2,0,1:T(4,128)S(1)}, f32[3,128,1]{2,0,1:T(4,128)S(1)}, u32[]{:S(2)}, u32[]{:S(2)}) %collective-permute-start.7) | collective-permute-done | bytes 1568 | tf_op jit(solution)/shard_map/ppermute | solution.py:35
  57.8 7.1 %collective-permute-start.9 = (f32[1,128,128]{2,0,1:T(1,128)S(1)}, f32[1,128,128]{2,0,1:T(1,128)S(1)}, u32[]{:S(2)}, u32[]{:S(2)}) collective-permute-start(f32[1,128,128]{2,0,1:T(1,128)S(1)} %get-tuple-element.60), channel_id=1, source_target_pairs={{8,0},{16,8},{24,16},{32,24},{40,32},{48,40},{56,48},{64,56},{72,6... | collective-permute-start | bytes 196616 | tf_op jit(solution)/shard_map/ppermute | solution.py:35
  66.8 7.3 %collective-permute-done.8 = f32[1,128,128]{2,0,1:T(1,128)S(1)} collective-permute-done((f32[1,128,128]{2,0,1:T(1,128)S(1)}, f32[1,128,128]{2,0,1:T(1,128)S(1)}, u32[]{:S(2)}, u32[]{:S(2)}) %collective-permute-start.8) | collective-permute-done | bytes 65568 | tf_op jit(solution)/shard_map/ppermute | solution.py:33
  94.1 7.3 %collective-permute-done.12 = f32[1,128,128]{2,0,1:T(1,128)S(1)} collective-permute-done((f32[1,128,128]{2,0,1:T(1,128)S(1)}, f32[1,128,128]{2,0,1:T(1,128)S(1)}, u32[]{:S(2)}, u32[]{:S(2)}) %collective-permute-start.12) | collective-permute-done | bytes 65568 | tf_op jit(solution)/shard_map/ppermute | solution.py:33
  121.6 7.0 %collective-permute-done.16 = f32[1,128,128]{2,0,1:T(1,128)S(1)} collective-permute-done((f32[1,128,128]{2,0,1:T(1,128)S(1)}, f32[1,128,128]{2,0,1:T(1,128)S(1)}, u32[]{:S(2)}, u32[]{:S(2)}) %collective-permute-start.16) | collective-permute-done | bytes 65568 | tf_op jit(solution)/shard_map/ppermute | solution.py:33
  148.6 7.3 %collective-permute-done.20 = f32[1,128,128]{2,0,1:T(1,128)S(1)} collective-permute-done((f32[1,128,128]{2,0,1:T(1,128)S(1)}, f32[1,128,128]{2,0,1:T(1,128)S(1)}, u32[]{:S(2)}, u32[]{:S(2)}) %collective-permute-start.20) | collective-permute-done | bytes 65568 | tf_op jit(solution)/shard_map/ppermute | solution.py:33
  175.8 7.3 %collective-permute-done.24 = f32[1,128,128]{2,0,1:T(1,128)S(1)} collective-permute-done((f32[1,128,128]{2,0,1:T(1,128)S(1)}, f32[1,128,128]{2,0,1:T(1,128)S(1)}, u32[]{:S(2)}, u32[]{:S(2)}) %collective-permute-start.24) | collective-permute-done | bytes 65568 | tf_op jit(solution)/shard_map/ppermute | solution.py:33
  203.1 7.3 %collective-permute-done.28 = f32[1,128,128]{2,0,1:T(1,128)S(1)} collective-permute-done((f32[1,128,128]{2,0,1:T(1,128)S(1)}, f32[1,128,128]{2,0,1:T(1,128)S(1)}, u32[]{:S(2)}, u32[]{:S(2)}) %collective-permute-start.28) | collective-permute-done | bytes 65568 | tf_op jit(solution)/shard_map/ppermute | solution.py:33
  230.3 7.3 %collective-permute-done.32 = f32[1,128,128]{2,0,1:T(1,128)S(1)} collective-permute-done((f32[1,128,128]{2,0,1:T(1,128)S(1)}, f32[1,128,128]{2,0,1:T(1,128)S(1)}, u32[]{:S(2)}, u32[]{:S(2)}) %collective-permute-start.32) | collective-permute-done | bytes 65568 | tf_op jit(solution)/shard_map/ppermute | solution.py:33
  240.2 4.9 collective-permute-start.35
  262.9 7.3 %collective-permute-start.38 = (f32[1,128,128]{2,0,1:T(1,128)S(1)}, f32[1,128,128]{2,0,1:T(1,128)S(1)}, u32[]{:S(2)}, u32[]{:S(2)}) collective-permute-start(f32[1,128,128]{2,0,1:T(1,128)S(1)} %get-tuple-element.58), channel_id=1, source_target_pairs={{8,0},{16,8},{24,16},{32,24},{40,32},{48,40},{56,48},{64,56},{72,6... | collective-permute-start | bytes 196616 | tf_op jit(solution)/shard_map/ppermute | solution.py:35
  279.9 5.0 collective-permute-start.42
  285.0 6.0 %collective-permute-done.43 = f32[3,128,1]{2,0,1:T(4,128)S(1)} collective-permute-done((f32[3,128,1]{2,0,1:T(4,128)S(1)}, f32[3,128,1]{2,0,1:T(4,128)S(1)}, u32[]{:S(2)}, u32[]{:S(2)}) %collective-permute-start.43) | collective-permute-done | bytes 1568 | tf_op jit(solution)/shard_map/ppermute | solution.py:35
  303.8 7.1 %collective-permute-start.45 = (f32[1,128,128]{2,0,1:T(1,128)S(1)}, f32[1,128,128]{2,0,1:T(1,128)S(1)}, u32[]{:S(2)}, u32[]{:S(2)}) collective-permute-start(f32[1,128,128]{2,0,1:T(1,128)S(1)} %get-tuple-element.17), channel_id=1, source_target_pairs={{8,0},{16,8},{24,16},{32,24},{40,32},{48,40},{56,48},{64,56},{72,6... | collective-permute-start | bytes 196616 | tf_op jit(solution)/shard_map/ppermute | solution.py:35
  312.9 7.3 %collective-permute-done.44 = f32[1,128,128]{2,0,1:T(1,128)S(1)} collective-permute-done((f32[1,128,128]{2,0,1:T(1,128)S(1)}, f32[1,128,128]{2,0,1:T(1,128)S(1)}, u32[]{:S(2)}, u32[]{:S(2)}) %collective-permute-start.44) | collective-permute-done | bytes 65568 | tf_op jit(solution)/shard_map/ppermute | solution.py:33
  340.2 7.3 %collective-permute-done.48 = f32[1,128,128]{2,0,1:T(1,128)S(1)} collective-permute-done((f32[1,128,128]{2,0,1:T(1,128)S(1)}, f32[1,128,128]{2,0,1:T(1,128)S(1)}, u32[]{:S(2)}, u32[]{:S(2)}) %collective-permute-start.48) | collective-permute-done | bytes 65568 | tf_op jit(solution)/shard_map/ppermute | solution.py:33
  367.4 7.3 %collective-permute-done.52 = f32[1,128,128]{2,0,1:T(1,128)S(1)} collective-permute-done((f32[1,128,128]{2,0,1:T(1,128)S(1)}, f32[1,128,128]{2,0,1:T(1,128)S(1)}, u32[]{:S(2)}, u32[]{:S(2)}) %collective-permute-start.52) | collective-permute-done | bytes 65568 | tf_op jit(solution)/shard_map/ppermute | solution.py:33
  394.6 7.3 %collective-permute-done.56 = f32[1,128,128]{2,0,1:T(1,128)S(1)} collective-permute-done((f32[1,128,128]{2,0,1:T(1,128)S(1)}, f32[1,128,128]{2,0,1:T(1,128)S(1)}, u32[]{:S(2)}, u32[]{:S(2)}) %collective-permute-start.56) | collective-permute-done | bytes 65568 | tf_op jit(solution)/shard_map/ppermute | solution.py:33
  421.9 7.3 %collective-permute-done.60 = f32[1,128,128]{2,0,1:T(1,128)S(1)} collective-permute-done((f32[1,128,128]{2,0,1:T(1,128)S(1)}, f32[1,128,128]{2,0,1:T(1,128)S(1)}, u32[]{:S(2)}, u32[]{:S(2)}) %collective-permute-start.60) | collective-permute-done | bytes 65568 | tf_op jit(solution)/shard_map/ppermute | solution.py:33
  445.2 5.4 all-to-all-start.1
  455.8 5.7 all-to-all-start.3
  463.5 7.3 %collective-permute-start.75 = (f32[1,16,1024]{2,1,0:T(8,128)S(1)}, f32[1,16,1024]{2,1,0:T(8,128)S(1)}, u32[]{:S(2)}, u32[]{:S(2)}) collective-permute-start(f32[1,16,1024]{2,1,0:T(8,128)S(1)} %all_to_all.68), channel_id=1, source_target_pairs={{8,0},{16,8},{24,16},{32,24},{40,32},{48,40},{56,48},{64,56},{72,6... | collective-permute-start | bytes 196616 | tf_op jit(solution)/shard_map/ppermute | solution.py:35
  486.0 6.0 %collective-permute-start.69 = (f32[1,128,128]{2,0,1:T(1,128)S(1)}, f32[1,128,128]{2,0,1:T(1,128)S(1)}, u32[]{:S(2)}, u32[]{:S(2)}) collective-permute-start(f32[1,128,128]{2,0,1:T(1,128)S(1)} %add_multiply_fusion.1), channel_id=1, source_target_pairs={{8,0},{16,8},{24,16},{32,24},{40,32},{48,40},{56,48},{64,56},{72,6... | collective-permute-start | bytes 196616 | tf_op jit(solution)/shard_map/ppermute | solution.py:35
  494.0 7.2 %collective-permute-done.68 = f32[1,128,128]{2,0,1:T(1,128)S(1)} collective-permute-done((f32[1,128,128]{2,0,1:T(1,128)S(1)}, f32[1,128,128]{2,0,1:T(1,128)S(1)}, u32[]{:S(2)}, u32[]{:S(2)}) %collective-permute-start.68) | collective-permute-done | bytes 65568 | tf_op jit(solution)/shard_map/ppermute | solution.py:33
  519.2 6.0 %all-to-all-start.2 = ((f32[1,128,128]{2,0,1:T(1,128)}), f32[1,128,128]{2,0,1:T(1,128)S(1)}, u32[]{:S(2)}, u32[]{:S(2)}) async-start(f32[1,128,128]{2,0,1:T(1,128)} %get-tuple-element.12), calls=%async_computation.2 | async-start | bytes 131072 | tf_op jit(solution)/shard_map/all_to_all | solution.py:209
  533.7 6.6 %all-to-all-start.4 = ((f32[1,128,128]{2,0,1:T(1,128)}), f32[1,128,128]{2,0,1:T(1,128)S(1)}, u32[]{:S(2)}, u32[]{:S(2)}) async-start(f32[1,128,128]{2,0,1:T(1,128)} %bitcast.201), calls=%async_computation.4 | async-start | bytes 131072 | tf_op jit(solution)/shard_map/all_to_all | solution.py:210
  540.3 6.1 %collective-permute-start.74 = (f32[1,16,1024]{2,1,0:T(8,128)S(1)}, f32[1,16,1024]{2,1,0:T(8,128)S(1)}, u32[]{:S(2)}, u32[]{:S(2)}) collective-permute-start(f32[1,16,1024]{2,1,0:T(8,128)S(1)} %all_to_all.76), channel_id=1, source_target_pairs={{8,0},{16,8},{24,16},{32,24},{40,32},{48,40},{56,48},{64,56},{72,6... | collective-permute-start | bytes 196616 | tf_op jit(solution)/shard_map/ppermute | solution.py:35
  559.6 5.3 collective-permute-start.81
  566.8 7.3 %collective-permute-done.80 = f32[1,16,1024]{2,1,0:T(8,128)S(1)} collective-permute-done((f32[1,16,1024]{2,1,0:T(8,128)S(1)}, f32[1,16,1024]{2,1,0:T(8,128)S(1)}, u32[]{:S(2)}, u32[]{:S(2)}) %collective-permute-start.80) | collective-permute-done | bytes 65568 | tf_op jit(solution)/shard_map/ppermute | solution.py:33
  (615 shorter events, 366.6 us)
Async XLA Ops:
  0.6 23.9 %collective-permute-start.3 = (f32[1,128,128]{2,0,1:T(1,128)}, f32[1,128,128]{2,0,1:T(1,128)S(1)}, u32[]{:S(2)}, u32[]{:S(2)}) collective-permute-start(f32[1,128,128]{2,0,1:T(1,128)} %bitcast.314), channel_id=1, source_target_pairs={{8,0},{16,8},{24,16},{32,24},{40,32},{48,40},{56,48},{64,56},{72,6... | collective-permute-start | bytes 196616 | tf_op jit(solution)/shard_map/ppermute | solution.py:35
  7.6 17.0 %collective-permute-start.1 = (f32[1,128,128]{2,0,1:T(1,128)}, f32[1,128,128]{2,0,1:T(1,128)S(1)}, u32[]{:S(2)}, u32[]{:S(2)}) collective-permute-start(f32[1,128,128]{2,0,1:T(1,128)} %bitcast.315), channel_id=1, source_target_pairs={{0,8},{8,16},{16,24},{24,32},{32,40},{40,48},{48,56},{56,64},{64,7... | collective-permute-start | bytes 196616 | tf_op jit(solution)/shard_map/ppermute | solution.py:33
  15.1 16.6 %collective-permute-start = (f32[1,128,128]{2,0,1:T(1,128)S(1)}, f32[1,128,128]{2,0,1:T(1,128)S(1)}, u32[]{:S(2)}, u32[]{:S(2)}) collective-permute-start(f32[1,128,128]{2,0,1:T(1,128)S(1)} %get-tuple-element.104), channel_id=1, source_target_pairs={{0,8},{8,16},{16,24},{24,32},{32,40},{40,48},{48,56},{56,64},{64,7... | collective-permute-start | bytes 196616 | tf_op jit(solution)/shard_map/ppermute | solution.py:33
  17.2 14.6 %collective-permute-start.2 = (f32[1,128,128]{2,0,1:T(1,128)S(1)}, f32[1,128,128]{2,0,1:T(1,128)S(1)}, u32[]{:S(2)}, u32[]{:S(2)}) collective-permute-start(f32[1,128,128]{2,0,1:T(1,128)S(1)} %get-tuple-element.104), channel_id=1, source_target_pairs={{8,0},{16,8},{24,16},{32,24},{40,32},{48,40},{56,48},{64,56},{72,6... | collective-permute-start | bytes 196616 | tf_op jit(solution)/shard_map/ppermute | solution.py:35
  25.0 14.2 %collective-permute-start.5 = (f32[3,128,1]{2,0,1:T(4,128)S(1)}, f32[3,128,1]{2,0,1:T(4,128)S(1)}, u32[]{:S(2)}, u32[]{:S(2)}) collective-permute-start(f32[3,128,1]{2,0,1:T(4,128)S(1)} %get-tuple-element.144), channel_id=1, source_target_pairs={{0,1},{1,2},{2,3},{3,4},{4,5},{5,6},{6,7},{8,9},{9,10},{10,11},{11... | collective-permute-start | bytes 4616 | tf_op jit(solution)/shard_map/ppermute | solution.py:33
  29.1 16.3 %collective-permute-start.7 = (f32[3,128,1]{2,0,1:T(4,128)S(1)}, f32[3,128,1]{2,0,1:T(4,128)S(1)}, u32[]{:S(2)}, u32[]{:S(2)}) collective-permute-start(f32[3,128,1]{2,0,1:T(4,128)S(1)} %get-tuple-element.145), channel_id=1, source_target_pairs={{1,0},{2,1},{3,2},{4,3},{5,4},{6,5},{7,6},{9,8},{10,9},{11,10},{12... | collective-permute-start | bytes 4616 | tf_op jit(solution)/shard_map/ppermute | solution.py:35
  32.3 13.4 %collective-permute-start.4 = (f32[3,128,1]{2,0,1:T(4,128)S(1)}, f32[3,128,1]{2,0,1:T(4,128)S(1)}, u32[]{:S(2)}, u32[]{:S(2)}) collective-permute-start(f32[3,128,1]{2,0,1:T(4,128)S(1)} %get-tuple-element.143), channel_id=1, source_target_pairs={{0,1},{1,2},{2,3},{3,4},{4,5},{5,6},{6,7},{8,9},{9,10},{10,11},{11... | collective-permute-start | bytes 4616 | tf_op jit(solution)/shard_map/ppermute | solution.py:33
  35.5 12.7 %collective-permute-start.6 = (f32[3,128,1]{2,0,1:T(4,128)S(1)}, f32[3,128,1]{2,0,1:T(4,128)S(1)}, u32[]{:S(2)}, u32[]{:S(2)}) collective-permute-start(f32[3,128,1]{2,0,1:T(4,128)S(1)} %get-tuple-element.142), channel_id=1, source_target_pairs={{1,0},{2,1},{3,2},{4,3},{5,4},{6,5},{7,6},{9,8},{10,9},{11,10},{12... | collective-permute-start | bytes 4616 | tf_op jit(solution)/shard_map/ppermute | solution.py:35
  76.7 9.7 %collective-permute-start.11 = (f32[3,128,1]{2,0,1:T(4,128)S(1)}, f32[3,128,1]{2,0,1:T(4,128)S(1)}, u32[]{:S(2)}, u32[]{:S(2)}) collective-permute-start(f32[3,128,1]{2,0,1:T(4,128)S(1)} %get-tuple-element.141), channel_id=1, source_target_pairs={{1,0},{2,1},{3,2},{4,3},{5,4},{6,5},{7,6},{9,8},{10,9},{11,10},{12... | collective-permute-start | bytes 4616 | tf_op jit(solution)/shard_map/ppermute | solution.py:35
  255.2 15.0 %collective-permute-start.39 = (f32[1,128,128]{2,0,1:T(1,128)S(1)}, f32[1,128,128]{2,0,1:T(1,128)S(1)}, u32[]{:S(2)}, u32[]{:S(2)}) collective-permute-start(f32[1,128,128]{2,0,1:T(1,128)S(1)} %get-tuple-element.59), channel_id=1, source_target_pairs={{8,0},{16,8},{24,16},{32,24},{40,32},{48,40},{56,48},{64,56},{72,6... | collective-permute-start | bytes 196616 | tf_op jit(solution)/shard_map/ppermute | solution.py:35
  259.0 11.2 %collective-permute-start.37 = (f32[1,128,128]{2,0,1:T(1,128)S(1)}, f32[1,128,128]{2,0,1:T(1,128)S(1)}, u32[]{:S(2)}, u32[]{:S(2)}) collective-permute-start(f32[1,128,128]{2,0,1:T(1,128)S(1)} %get-tuple-element.59), channel_id=1, source_target_pairs={{0,8},{8,16},{16,24},{24,32},{32,40},{40,48},{48,56},{56,64},{64,7... | collective-permute-start | bytes 196616 | tf_op jit(solution)/shard_map/ppermute | solution.py:33
  261.0 16.4 %collective-permute-start.36 = (f32[1,128,128]{2,0,1:T(1,128)S(1)}, f32[1,128,128]{2,0,1:T(1,128)S(1)}, u32[]{:S(2)}, u32[]{:S(2)}) collective-permute-start(f32[1,128,128]{2,0,1:T(1,128)S(1)} %get-tuple-element.58), channel_id=1, source_target_pairs={{0,8},{8,16},{16,24},{24,32},{32,40},{40,48},{48,56},{56,64},{64,7... | collective-permute-start | bytes 196616 | tf_op jit(solution)/shard_map/ppermute | solution.py:33
  262.9 14.5 %collective-permute-start.38 = (f32[1,128,128]{2,0,1:T(1,128)S(1)}, f32[1,128,128]{2,0,1:T(1,128)S(1)}, u32[]{:S(2)}, u32[]{:S(2)}) collective-permute-start(f32[1,128,128]{2,0,1:T(1,128)S(1)} %get-tuple-element.58), channel_id=1, source_target_pairs={{8,0},{16,8},{24,16},{32,24},{40,32},{48,40},{56,48},{64,56},{72,6... | collective-permute-start | bytes 196616 | tf_op jit(solution)/shard_map/ppermute | solution.py:35
  270.7 14.2 %collective-permute-start.41 = (f32[3,128,1]{2,0,1:T(4,128)S(1)}, f32[3,128,1]{2,0,1:T(4,128)S(1)}, u32[]{:S(2)}, u32[]{:S(2)}) collective-permute-start(f32[3,128,1]{2,0,1:T(4,128)S(1)} %get-tuple-element.126), channel_id=1, source_target_pairs={{0,1},{1,2},{2,3},{3,4},{4,5},{5,6},{6,7},{8,9},{9,10},{10,11},{11... | collective-permute-start | bytes 4616 | tf_op jit(solution)/shard_map/ppermute | solution.py:33
  272.9 18.1 %collective-permute-start.43 = (f32[3,128,1]{2,0,1:T(4,128)S(1)}, f32[3,128,1]{2,0,1:T(4,128)S(1)}, u32[]{:S(2)}, u32[]{:S(2)}) collective-permute-start(f32[3,128,1]{2,0,1:T(4,128)S(1)} %get-tuple-element.127), channel_id=1, source_target_pairs={{1,0},{2,1},{3,2},{4,3},{5,4},{6,5},{7,6},{9,8},{10,9},{11,10},{12... | collective-permute-start | bytes 4616 | tf_op jit(solution)/shard_map/ppermute | solution.py:35
  278.0 13.4 %collective-permute-start.40 = (f32[3,128,1]{2,0,1:T(4,128)S(1)}, f32[3,128,1]{2,0,1:T(4,128)S(1)}, u32[]{:S(2)}, u32[]{:S(2)}) collective-permute-start(f32[3,128,1]{2,0,1:T(4,128)S(1)} %get-tuple-element.125), channel_id=1, source_target_pairs={{0,1},{1,2},{2,3},{3,4},{4,5},{5,6},{6,7},{8,9},{9,10},{10,11},{11... | collective-permute-start | bytes 4616 | tf_op jit(solution)/shard_map/ppermute | solution.py:33
  279.9 14.0 %collective-permute-start.42 = (f32[3,128,1]{2,0,1:T(4,128)S(1)}, f32[3,128,1]{2,0,1:T(4,128)S(1)}, u32[]{:S(2)}, u32[]{:S(2)}) collective-permute-start(f32[3,128,1]{2,0,1:T(4,128)S(1)} %get-tuple-element.124), channel_id=1, source_target_pairs={{1,0},{2,1},{3,2},{4,3},{5,4},{6,5},{7,6},{9,8},{10,9},{11,10},{12... | collective-permute-start | bytes 4616 | tf_op jit(solution)/shard_map/ppermute | solution.py:35
  322.7 9.8 %collective-permute-start.47 = (f32[3,128,1]{2,0,1:T(4,128)S(1)}, f32[3,128,1]{2,0,1:T(4,128)S(1)}, u32[]{:S(2)}, u32[]{:S(2)}) collective-permute-start(f32[3,128,1]{2,0,1:T(4,128)S(1)} %get-tuple-element.123), channel_id=1, source_target_pairs={{1,0},{2,1},{3,2},{4,3},{5,4},{6,5},{7,6},{9,8},{10,9},{11,10},{12... | collective-permute-start | bytes 4616 | tf_op jit(solution)/shard_map/ppermute | solution.py:35
  429.5 11.7 %collective-permute-start.62 = (f32[3,128,1]{2,0,1:T(4,128)S(1)}, f32[3,128,1]{2,0,1:T(4,128)S(1)}, u32[]{:S(2)}, u32[]{:S(2)}) collective-permute-start(f32[3,128,1]{2,0,1:T(4,128)S(1)} %get-tuple-element.114), channel_id=1, source_target_pairs={{0,1},{1,2},{2,3},{3,4},{4,5},{5,6},{6,7},{8,9},{9,10},{10,11},{11... | collective-permute-start | bytes 4616 | tf_op jit(solution)/shard_map/ppermute | solution.py:33
  431.8 10.1 %collective-permute-start.63 = (f32[3,128,1]{2,0,1:T(4,128)S(1)}, f32[3,128,1]{2,0,1:T(4,128)S(1)}, u32[]{:S(2)}, u32[]{:S(2)}) collective-permute-start(f32[3,128,1]{2,0,1:T(4,128)S(1)} %get-tuple-element.115), channel_id=1, source_target_pairs={{1,0},{2,1},{3,2},{4,3},{5,4},{6,5},{7,6},{9,8},{10,9},{11,10},{12... | collective-permute-start | bytes 4616 | tf_op jit(solution)/shard_map/ppermute | solution.py:35
  445.2 9.9 %all-to-all-start.1 = ((f32[1,128,128]{2,0,1:T(1,128)}), f32[1,128,128]{2,0,1:T(1,128)S(1)}, u32[]{:S(2)}, u32[]{:S(2)}) async-start(f32[1,128,128]{2,0,1:T(1,128)} %get-tuple-element.500), calls=%async_computation.1 | async-start | bytes 131072 | tf_op jit(solution)/shard_map/all_to_all | solution.py:211
  450.8 20.1 %collective-permute-start.65 = (f32[1,128,128]{2,0,1:T(1,128)S(1)}, f32[1,128,128]{2,0,1:T(1,128)S(1)}, u32[]{:S(2)}, u32[]{:S(2)}) collective-permute-start(f32[1,128,128]{2,0,1:T(1,128)S(1)} %add_multiply_fusion.2), channel_id=1, source_target_pairs={{8,0},{16,8},{24,16},{32,24},{40,32},{48,40},{56,48},{64,56},{72,6... | collective-permute-start | bytes 196616 | tf_op jit(solution)/shard_map/ppermute | solution.py:35
  452.7 18.2 %collective-permute-start.64 = (f32[1,128,128]{2,0,1:T(1,128)S(1)}, f32[1,128,128]{2,0,1:T(1,128)S(1)}, u32[]{:S(2)}, u32[]{:S(2)}) collective-permute-start(f32[1,128,128]{2,0,1:T(1,128)S(1)} %add_multiply_fusion.2), channel_id=1, source_target_pairs={{0,8},{8,16},{16,24},{24,32},{32,40},{40,48},{48,56},{56,64},{64,7... | collective-permute-start | bytes 196616 | tf_op jit(solution)/shard_map/ppermute | solution.py:33
  455.8 15.0 %all-to-all-start.3 = ((f32[1,128,128]{2,0,1:T(1,128)}), f32[1,128,128]{2,0,1:T(1,128)S(1)}, u32[]{:S(2)}, u32[]{:S(2)}) async-start(f32[1,128,128]{2,0,1:T(1,128)} %broadcast_in_dim.112), calls=%async_computation.3 | async-start | bytes 131072 | tf_op jit(solution)/shard_map/all_to_all | solution.py:212
  461.6 17.5 %collective-permute-start.73 = (f32[1,16,1024]{2,1,0:T(8,128)S(1)}, f32[1,16,1024]{2,1,0:T(8,128)S(1)}, u32[]{:S(2)}, u32[]{:S(2)}) collective-permute-start(f32[1,16,1024]{2,1,0:T(8,128)S(1)} %all_to_all.68), channel_id=1, source_target_pairs={{0,8},{8,16},{16,24},{24,32},{32,40},{40,48},{48,56},{56,64},{64,7... | collective-permute-start | bytes 196616 | tf_op jit(solution)/shard_map/ppermute | solution.py:33
  463.5 45.6 %collective-permute-start.75 = (f32[1,16,1024]{2,1,0:T(8,128)S(1)}, f32[1,16,1024]{2,1,0:T(8,128)S(1)}, u32[]{:S(2)}, u32[]{:S(2)}) collective-permute-start(f32[1,16,1024]{2,1,0:T(8,128)S(1)} %all_to_all.68), channel_id=1, source_target_pairs={{8,0},{16,8},{24,16},{32,24},{40,32},{48,40},{56,48},{64,56},{72,6... | collective-permute-start | bytes 196616 | tf_op jit(solution)/shard_map/ppermute | solution.py:35
  504.5 10.0 %collective-permute-start.71 = (f32[3,128,1]{2,0,1:T(4,128)}, f32[3,128,1]{2,0,1:T(4,128)S(1)}, u32[]{:S(2)}, u32[]{:S(2)}) collective-permute-start(f32[3,128,1]{2,0,1:T(4,128)} %get-tuple-element.111), channel_id=1, source_target_pairs={{1,0},{2,1},{3,2},{4,3},{5,4},{6,5},{7,6},{9,8},{10,9},{11,10},{12... | collective-permute-start | bytes 4616 | tf_op jit(solution)/shard_map/ppermute | solution.py:35
  519.2 11.9 %all-to-all-start.2 = ((f32[1,128,128]{2,0,1:T(1,128)}), f32[1,128,128]{2,0,1:T(1,128)S(1)}, u32[]{:S(2)}, u32[]{:S(2)}) async-start(f32[1,128,128]{2,0,1:T(1,128)} %get-tuple-element.12), calls=%async_computation.2 | async-start | bytes 131072 | tf_op jit(solution)/shard_map/all_to_all | solution.py:209
  525.2 29.3 %collective-permute-start.79 = (f32[3,1,1024]{2,1,0:T(1,128)S(1)}, f32[3,1,1024]{2,1,0:T(1,128)S(1)}, u32[]{:S(2)}, u32[]{:S(2)}) collective-permute-start(f32[3,1,1024]{2,1,0:T(1,128)S(1)} %get-tuple-element.151), channel_id=1, source_target_pairs={{1,0},{2,1},{3,2},{4,3},{5,4},{6,5},{7,6},{9,8},{10,9},{11,10},{12... | collective-permute-start | bytes 36872 | tf_op jit(solution)/shard_map/ppermute | solution.py:35
  528.9 25.7 %collective-permute-start.77 = (f32[3,1,1024]{2,1,0:T(1,128)S(1)}, f32[3,1,1024]{2,1,0:T(1,128)S(1)}, u32[]{:S(2)}, u32[]{:S(2)}) collective-permute-start(f32[3,1,1024]{2,1,0:T(1,128)S(1)} %get-tuple-element.150), channel_id=1, source_target_pairs={{0,1},{1,2},{2,3},{3,4},{4,5},{5,6},{6,7},{8,9},{9,10},{10,11},{11... | collective-permute-start | bytes 36872 | tf_op jit(solution)/shard_map/ppermute | solution.py:33
  531.1 15.3 %collective-permute-start.72 = (f32[1,16,1024]{2,1,0:T(8,128)S(1)}, f32[1,16,1024]{2,1,0:T(8,128)S(1)}, u32[]{:S(2)}, u32[]{:S(2)}) collective-permute-start(f32[1,16,1024]{2,1,0:T(8,128)S(1)} %all_to_all.76), channel_id=1, source_target_pairs={{0,8},{8,16},{16,24},{24,32},{32,40},{40,48},{48,56},{56,64},{64,7... | collective-permute-start | bytes 196616 | tf_op jit(solution)/shard_map/ppermute | solution.py:33
  533.7 21.0 %all-to-all-start.4 = ((f32[1,128,128]{2,0,1:T(1,128)}), f32[1,128,128]{2,0,1:T(1,128)S(1)}, u32[]{:S(2)}, u32[]{:S(2)}) async-start(f32[1,128,128]{2,0,1:T(1,128)} %bitcast.201), calls=%async_computation.4 | async-start | bytes 131072 | tf_op jit(solution)/shard_map/all_to_all | solution.py:210
  (62 other events, 506.8 us)
where the time goes:
time: 592 us; the launch traced here: 584 us
  starting transfers between devices  314 us (53%)
  waiting for transfers between devices  194 us (33%)
  other arithmetic  48.5 us (8%)
  local copies, waits for them, and re-layouts  22.2 us (4%)
    ppermute x42, starting transfers between devices, extended(): lax.ppermute(head, axis, [((i + 1) % count, i) for i in range(ends)])  193 us
    ppermute x42, waiting for transfers between devices, extended(): lax.ppermute(tail, axis, [(i, (i + 1) % count) for i in range(ends)])  139 us
    ppermute x42, starting transfers between devices, extended(): lax.ppermute(tail, axis, [(i, (i + 1) % count) for i in range(ends)])  92.7 us
    ppermute x42, waiting for transfers between devices, extended(): lax.ppermute(head, axis, [((i + 1) % count, i) for i in range(ends)])  53.5 us
    add x96, other arithmetic, apply_factors(): source + left_mult * shift_down(source, stride, 0.0)  16 us
  transfers between devices with their start and end apart: 89, of which 49 were waited for; matrix products, arithmetic and copies ran while one was open for 3% of the time, Pallas kernels for 0%

commit v1 on v0

v1 whole, which is shorter than its diff:
```python
import jax
import jax.numpy as jnp
from jax import lax
from jax.experimental import pallas as pl
from jax.experimental.pallas import tpu as pltpu
from jax.sharding import PartitionSpec as P

SWEEPS = 8
TABLE = (
    (4.0, 2.5, 1.2, 0.8),
    (2.4, 1.9, 1.6, 1.4),
    (0.05, 0.08, 0.1, 0.12),
    (0.38, 0.42, 0.45, 0.4),
    (5.0, 2.0, 0.6, 0.2),
)
FLOW_STEP = 2.0
STORAGE_TERM = 0.01
COND_FLOOR = 0.001
IRRIGATION = 0.3
GAS_STEP = 0.25

NX, NYD, LANES, DEPTH, SEG, SUB = 32, 8, 128, 128, 16, 8
COLS = LANES // NX
STRIPS = NX * NYD
REGION = 5
MESH = pl.DeviceIdType.MESH

FWD = 0
BACK = 30
SCALE = 60
LAST = 67
NFAC = 74


def levels():
    result = []
    kept = list(range(SEG))
    place = 0
    scale = 0
    step = 1
    while len(kept) > 1:
        gone, stay = kept[0::2], kept[1::2]
        result.append((step, gone, stay, place, scale))
        place += len(gone)
        if step > 1:
            scale += len(gone)
        kept = stay
        step *= 2
    return result


LEVELS = levels()


def rows(j):
    return pl.ds(SUB * j, SUB)


def roll(x, shift, axis):
    return pltpu.roll(x, shift % x.shape[axis], axis)


def sel(masks, values):
    return jnp.where(
        masks[0],
        jnp.float32(values[0]),
        jnp.where(
            masks[1],
            jnp.float32(values[1]),
            jnp.where(masks[2], jnp.float32(values[2]), jnp.float32(values[3])),
        ),
    )


def zone_masks(zone):
    return (zone < 0.5, zone < 1.5, zone < 2.5)


def saturation(head, masks):
    a, n, r, s, k = TABLE
    au = sel(masks, a) * jnp.maximum(-head, 1e-37)
    power = jnp.exp2(sel(masks, [v - 1.0 for v in n]) * jnp.log2(au))
    one_p = 1.0 + power * au
    log_p = jnp.log2(one_p)
    m = sel(masks, [1.0 - 1.0 / v for v in n])
    return power, one_p, m * log_p


def harmonic(u, v):
    return 2.0 * u * v / (u + v)


def kernel(
    head_ref, zone_ref, em_ref, oxy_ref, sul_ref, flux_ref,
    head_out, oxy_out,
    tmp, tmp2, send_a, recv_a, send_b, recv_b, send_x, recv_x, reg_a, reg_b, reg_c, reg_d,
    cond, half_cap, se_old, base, lat, fac, x, gas_g, gas_f, gas_c, gas_r,
    send_h, recv_h, send_o, recv_o, brick,
    sems, halo_s, halo_r,
):
    g = lax.axis_index("gx")
    y = lax.axis_index("gy")

    def strip_of(gx):
        return gx + (gx // 16) * (47 - 2 * gx)

    s = strip_of(g)
    me = y * NX + s

    def device_of(strip):
        return (strip_of(strip % NX), strip // NX)

    lane = lax.broadcasted_iota(jnp.int32, (SUB, LANES), 1)
    sub = lax.broadcasted_iota(jnp.int32, (SUB, LANES), 0)
    plane = lane % NX
    col = lane // NX
    first_plane, last_plane = plane == 0, plane == NX - 1
    first_col, last_col = col == 0, col == COLS - 1
    top, bottom = sub == 0, sub == SUB - 1

    barrier = pltpu.get_barrier_semaphore()

    def greet_x(k, c):
        pl.semaphore_signal(barrier, inc=1, device_id=((g + k) % NX, y), device_id_type=MESH)
        return c

    def greet_y(k, c):
        pl.semaphore_signal(barrier, inc=1, device_id=(g, (y + k) % NYD), device_id_type=MESH)
        return c

    def valid(k):
        return jnp.logical_and(me + k >= 0, me + k < STRIPS)

    lax.fori_loop(1, NX, greet_x, 0)
    lax.fori_loop(1, NYD, greet_y, 0)
    for k in (-1, 1, -2, 2):
        @pl.when(jnp.logical_and(valid(k), jnp.logical_or(s + k < 0, s + k >= NX)))
        def _():
            pl.semaphore_signal(barrier, inc=1, device_id=device_of(me + k), device_id_type=MESH)

    def pack(first, second, out):
        for q in range(NX // 2):
            f = first[8 * q : 8 * q + 8]
            t = second[8 * q : 8 * q + 8]
            out[pl.ds(16 * q, 8), :] = jnp.where(sub < 4, f, roll(t, 4, 0))
            out[pl.ds(16 * q + 8, 8), :] = jnp.where(sub < 4, roll(f, 4, 0), t)

    def segmented(ref):
        return jnp.concatenate(
            [ref[0, pl.ds(j, SUB, stride=SEG), :].astype(jnp.float32) for j in range(SEG)], axis=0
        ).T

    pack(segmented(head_ref), segmented(zone_ref), send_a)
    send_x[0:1, :] = em_ref[...].astype(jnp.float32)
    send_x[1:2, :] = flux_ref[...]
    own = pl.ds(pl.multiple_of(8 * g, 8), 8)
    recv_a[own, :] = send_a[pl.ds(pl.multiple_of(8 * s, 8), 8), :]
    recv_x[g] = send_x[...]

    lower = (2 - jnp.minimum(s, 2)) * jnp.minimum(y, 1)
    upper = (2 - jnp.minimum(NX - 1 - s, 2)) * jnp.minimum(NYD - 1 - y, 1)
    pl.semaphore_wait(barrier, NX - 1 + NYD - 1 + lower + upper)

    def remote(src, dst, ssem, rsem, device):
        return pltpu.make_async_remote_copy(
            src_ref=src, dst_ref=dst, send_sem=ssem, recv_sem=rsem, device_id=device, device_id_type=MESH
        )

    def scatter8(src, dst, index):
        def body(k, c):
            tg = (g + k) % NX
            remote(
                src.at[pl.ds(pl.multiple_of(8 * strip_of(tg), 8), 8)],
                dst.at[pl.ds(pl.multiple_of(8 * g, 8), 8)],
                sems.at[0, index],
                sems.at[1, index],
                (tg, y),
            ).start()
            return c

        lax.fori_loop(1, NX, body, 0)

    def wait_all(part, sem):
        pltpu.make_async_copy(part, part, sem).wait()

    scatter8(send_a, recv_a, 0)

    def body_x(k, c):
        tg = (g + k) % NX
        remote(send_x, recv_x.at[g], sems.at[0, 1], sems.at[1, 1], (tg, y)).start()
        return c

    lax.fori_loop(1, NX, body_x, 0)

    pack(segmented(oxy_ref), segmented(sul_ref), send_b)
    recv_b[own, :] = send_b[pl.ds(pl.multiple_of(8 * s, 8), 8), :]

    most8 = pl.ds(0, 8 * (NX - 1))
    wait_all(recv_a.at[most8], sems.at[1, 0])

    def unpack(src, field):
        parts = [
            src[pl.ds(64 * q + 4 * field + c, 8, stride=8), :] for c in range(COLS) for q in range(NX // 8)
        ]
        return jnp.concatenate(parts, axis=0).T

    reg_a[2, 0:128, :] = unpack(recv_a, 0)
    reg_a[2, 128:256, :] = unpack(recv_a, 1)
    wait_all(recv_x.at[pl.ds(0, NX - 1)], sems.at[1, 1])
    tmp[0:32, :] = recv_x[:, 0, :]
    tmp[32:64, :] = recv_x[:, 1, :]
    tmp[64:128, :] = jnp.zeros((64, LANES), jnp.float32)
    tmp2[...] = tmp[...].T
    emitted = jnp.zeros((1, LANES), jnp.float32)
    fluxes = jnp.zeros((1, LANES), jnp.float32)
    lane1 = lax.broadcasted_iota(jnp.int32, (1, LANES), 1) // NX
    for c in range(COLS):
        row = tmp2[pl.ds(4 * s + c, 1), :]
        emitted = jnp.where(lane1 == c, roll(row, 32 * c, 1), emitted)
        fluxes = jnp.where(lane1 == c, roll(row, 32 * c - 32, 1), fluxes)
    reg_a[2, 256:264, :] = jnp.concatenate(
        [emitted, fluxes, jnp.zeros((6, LANES), jnp.float32)], axis=0
    )

    def halo(reg, index, middle, ks, start):
        for k in ks:
            there = middle - k

            @pl.when(valid(k))
            def _():
                copy = remote(
                    reg.at[middle],
                    reg.at[there],
                    halo_s.at[index, middle + k],
                    halo_r.at[index, there],
                    device_of(me + k),
                )
                if start:
                    copy.start()
                else:
                    copy.wait_send()

    def arrive(reg, index, middle, b):
        strip = me + b - middle
        inside = jnp.logical_and(strip >= 0, strip < STRIPS)

        @pl.when(inside)
        def _():
            pltpu.make_async_copy(reg.at[b], reg.at[b], halo_r.at[index, b]).wait()

        @pl.when(jnp.logical_not(inside))
        def _():
            reg[b] = reg[middle]

    halo(reg_a, 0, 2, (-1, 1, -2, 2), True)
    scatter8(send_b, recv_b, 2)

    def picard(reg, index, first):
        def retain(i, carry):
            step = (i + 1) // 2
            b = 2 + step * (1 - 2 * (i % 2))

            @pl.when(i > 0)
            def _():
                arrive(reg, index, 2, b)

            for j in range(SEG):
                h = reg[b, rows(j), :]
                masks = zone_masks(reg_a[b, pl.ds(128 + 8 * j, 8), :])
                power, one_p, mlog = saturation(h, masks)
                se = jnp.exp2(-mlog)
                a, n, r, sat, kk = TABLE
                filled = power * se
                cap = (
                    sel(masks, [(w - v) * p * q * (1.0 - 1.0 / q) / FLOW_STEP for p, q, v, w in zip(a, n, r, sat)])
                    * filled
                    / one_p
                    + STORAGE_TERM / FLOW_STEP
                )
                rest = 1.0 - filled
                cond[b, rows(j), :] = sel(masks, kk) * (jnp.exp2(-0.5 * mlog) * rest * rest + COND_FLOOR)
                half_cap[b, rows(j), :] = cap
                x[0, b, rows(j), :] = h
                if first:
                    se_old[b, rows(j), :] = se
                    base[b, rows(j), :] = cap * h
                else:
                    base[b, rows(j), :] = cap * h - sel(
                        masks, [(w - v) / FLOW_STEP for v, w in zip(r, sat)]
                    ) * (se - se_old[b, rows(j), :])
            return carry

        lax.fori_loop(0, REGION, retain, 0)

        def assemble(b, carry):
            after, before = jnp.minimum(b + 1, REGION - 1), jnp.maximum(b - 1, 0)
            strip = me + b - 2
            closed = jnp.logical_or(strip == -1, strip == STRIPS - 1)
            open_face = jnp.where(closed, 0.0, 1.0)
            right_mask = jnp.where(last_col, open_face, 1.0)
            ks = [cond[b, rows(j), :] for j in range(SEG)]
            ups = [harmonic(ks[j], ks[j - 1]) for j in range(1, SEG)]
            up0 = jnp.where(top, 0.0, harmonic(ks[0], roll(ks[SEG - 1], 1, 0)))
            ups = [up0] + ups
            los = ups[1:] + [roll(up0, -1, 0)]
            av, cv = [], []
            for j in range(SEG):
                k = ks[j]
                xp = jnp.where(last_plane, 0.0, harmonic(k, roll(k, -1, 1)))
                xm = roll(xp, 1, 1)
                yp = right_mask * harmonic(
                    k, roll(jnp.where(first_col, cond[after, rows(j), :], k), -NX, 1)
                )
                lat[b, 3, rows(j), :] = yp
                ym = roll(jnp.where(last_col, lat[before, 3, rows(j), :], yp), NX, 1)
                diag = half_cap[b, rows(j), :] + xp + xm + yp + ym + ups[j] + los[j]
                inv = 1.0 / diag
                rhs = base[b, rows(j), :] + ups[j] - los[j]
                if j == SEG - 1:
                    rhs = rhs - jnp.where(bottom, k, 0.0)
                if j == 0:
                    rhs = rhs + jnp.where(top, IRRIGATION * reg_a[b, pl.ds(256, 1), :], 0.0)
                base[b, rows(j), :] = rhs * inv
                lat[b, 0, rows(j), :] = xm * inv
                lat[b, 1, rows(j), :] = xp * inv
                lat[b, 2, rows(j), :] = ym * inv
                lat[b, 4, rows(j), :] = yp * inv
                av.append(ups[j] * inv)
                cv.append(los[j] * inv)

            def put(i, value):
                fac[b, rows(i), :] = value

            bv = [None] * SEG
            for step, gone, stay, place, scale in LEVELS:
                for i, e in enumerate(gone):
                    if step > 1:
                        rec = 1.0 / bv[e]
                        put(SCALE + scale + i, rec)
                        av[e] = av[e] * rec
                        cv[e] = cv[e] * rec
                        bv[e] = rec
                    put(BACK + place + i, av[e])
                    put(BACK + 15 + place + i, cv[e])
                new = {}
                for i, j in enumerate(stay):
                    up, dn = j - step, j + step
                    if dn < SEG:
                        a_dn, c_dn = av[dn], cv[dn]
                        r_dn = bv[dn] if step > 1 else None
                    else:
                        a_dn, c_dn = roll(av[dn - SEG], -1, 0), roll(cv[dn - SEG], -1, 0)
                        r_dn = roll(bv[dn - SEG], -1, 0) if step > 1 else None
                    diag = (bv[j] if step > 1 else 1.0) - av[j] * cv[up] - cv[j] * a_dn
                    alpha = av[j] * bv[up] if step > 1 else av[j]
                    gamma = cv[j] * r_dn if step > 1 else cv[j]
                    put(FWD + place + i, alpha)
                    put(FWD + 15 + place + i, gamma)
                    new[j] = (av[j] * av[up], diag, cv[j] * c_dn)
                for j in stay:
                    av[j], bv[j], cv[j] = new[j]
            a, d, c = av[SEG - 1], bv[SEG - 1], cv[SEG - 1]
            for i, step in enumerate((1, 2, 4)):
                alpha = a / roll(d, step, 0)
                gamma = c / roll(d, -step, 0)
                put(LAST + 2 * i, alpha)
                put(LAST + 2 * i + 1, gamma)
                d = d - alpha * roll(c, step, 0) - gamma * roll(a, -step, 0)
                a, c = alpha * roll(a, step, 0), gamma * roll(c, -step, 0)
            put(LAST + 6, 1.0 / d)
            return carry

        lax.fori_loop(0, REGION, assemble, 0)

        def relax(now, b):
            def get(i):
                return fac[b, rows(i), :]

            later = 1 - now
            f = []
            for j in range(SEG):
                v = x[now, b, rows(j), :]
                left = jnp.where(last_col, x[now, max(b - 1, 0), rows(j), :], v)
                right = jnp.where(first_col, x[now, min(b + 1, REGION - 1), rows(j), :], v)
                f.append(
                    base[b, rows(j), :]
                    + lat[b, 0, rows(j), :] * roll(v, 1, 1)
                    + lat[b, 1, rows(j), :] * roll(v, -1, 1)
                    + lat[b, 2, rows(j), :] * roll(left, NX, 1)
                    + lat[b, 4, rows(j), :] * roll(right, -NX, 1)
                )
            for step, gone, stay, place, scale in LEVELS:
                for i, j in enumerate(stay):
                    dn = f[j + step] if j + step < SEG else roll(f[j + step - SEG], -1, 0)
                    f[j] = f[j] + get(FWD + place + i) * f[j - step] + get(FWD + 15 + place + i) * dn
            v = f[SEG - 1]
            for i, step in enumerate((1, 2, 4)):
                v = v + get(LAST + 2 * i) * roll(v, step, 0) + get(LAST + 2 * i + 1) * roll(v, -step, 0)
            f[SEG - 1] = v * get(LAST + 6)
            wrapped = roll(f[SEG - 1], 1, 0)
            for step, gone, stay, place, scale in reversed(LEVELS):
                for i, e in enumerate(gone):
                    up = f[e - step] if e >= step else wrapped
                    src = f[e] * get(SCALE + scale + i) if step > 1 else f[e]
                    f[e] = src + get(BACK + place + i) * up + get(BACK + 15 + place + i) * f[e + step]
            for j in range(SEG):
                x[later, b, rows(j), :] = f[j]

        def wide(t, carry):
            for b in range(REGION):
                relax(t % 2, b)
            return carry

        def narrow(t, carry):
            for b in (1, 2, 3):
                relax(t % 2, b)
            return carry

        lax.fori_loop(0, 3, wide, 0)
        lax.fori_loop(3, 7, narrow, 0)
        relax(1, 2)

    picard(reg_a, 0, True)
    reg_c[2] = x[0, 2]
    halo(reg_c, 1, 2, (-1, 1, -2, 2), True)

    wait_all(recv_b.at[most8], sems.at[1, 2])
    reg_b[1, 0:128, :] = unpack(recv_b, 0)
    reg_b[1, 128:256, :] = unpack(recv_b, 1)
    halo(reg_b, 3, 1, (-1, 1), True)

    picard(reg_c, 1, False)
    reg_d[1] = x[0, 2]
    halo(reg_d, 2, 1, (-1, 1), True)

    def scatter4(src, dst, index):
        def body(k, c):
            tg = (g + k) % NX
            remote(src.at[tg], dst.at[s], sems.at[0, index], sems.at[1, index], (tg, y)).start()
            return c

        lax.fori_loop(1, NX, body, 0)

    def pack_planes(field, out, own_slot):
        tmp[...] = field.T
        for p in range(NX):
            out[p] = tmp[pl.ds(p, COLS, stride=NX), :]
        own_slot[s] = out[g]

    pack_planes(x[0, 2], send_h, recv_h)
    scatter4(send_h, recv_h, 3)

    def gas_prepare(i, carry):
        b = (i + 1) % 3

        @pl.when(i > 0)
        def _():
            arrive(reg_b, 3, 1, b)
            arrive(reg_d, 2, 1, b)

        strip = me + b - 1
        inside = jnp.where(jnp.logical_and(strip >= 0, strip < STRIPS), 1.0, 0.0)
        a, n, r, sat, kk = TABLE
        for j in range(SEG):
            masks = zone_masks(reg_a[b + 1, pl.ds(128 + 8 * j, 8), :])
            power, one_p, mlog = saturation(reg_d[b, rows(j), :], masks)
            se = jnp.exp2(-mlog)
            span = sel(masks, [w - v for v, w in zip(r, sat)])
            inv_s = sel(masks, [1.0 / w for w in sat])
            gas = jnp.maximum(span * (1.0 - se), 1e-37)
            root = jnp.exp2((5.0 / 3.0) * jnp.log2(gas)) * inv_s * inside
            conc = reg_b[b, rows(j), :]
            gas_g[b, rows(j), :] = root
            gas_f[0, b, rows(j), :] = root * conc
            gas_c[0, b, rows(j), :] = conc
            gas_r[b, rows(j), :] = reg_b[b, pl.ds(128 + 8 * j, 8), :] * (sel(masks, r) + span * se) * inv_s
            gas_r[b, pl.ds(128 + 8 * j, 8), :] = GAS_STEP * inv_s
        return carry

    lax.fori_loop(0, 3, gas_prepare, 0)

    def gas_advance(step, b):
        before, after = jnp.maximum(b - 1, 0), jnp.minimum(b + 1, 2)

        def total(get, j):
            v = get(b, j)
            left = jnp.where(last_col, get(before, j), v)
            right = jnp.where(first_col, get(after, j), v)
            above = get(b, j - 1) if j > 0 else jnp.where(top, 0.0, roll(get(b, SEG - 1), 1, 0))
            below = get(b, j + 1) if j < SEG - 1 else jnp.where(bottom, 0.0, roll(get(b, 0), -1, 0))
            return (
                jnp.where(first_plane, 0.0, roll(v, 1, 1))
                + jnp.where(last_plane, 0.0, roll(v, -1, 1))
                + roll(left, NX, 1)
                + roll(right, -NX, 1)
                + above
                + below
            )

        flux = reg_a[b + 1, pl.ds(257, 1), :]
        for j in range(SEG):
            conc = gas_c[step, b, rows(j), :]
            root = gas_g[b, rows(j), :]
            sum_f = total(lambda bb, jj: gas_f[step, bb, rows(jj), :], j)
            sum_g = total(lambda bb, jj: gas_g[bb, rows(jj), :], j)
            if j < SEG - 1:
                under = gas_c[step, b, rows(j + 1), :]
            else:
                under = jnp.where(bottom, 1.0, roll(gas_c[step, b, rows(0), :], -1, 0))
            change = root * (sum_f - conc * sum_g) + flux * (under - conc) - gas_r[b, rows(j), :] * conc
            if j == 0:
                change = change + jnp.where(top, 2.0 * root * root * (1.0 - conc), 0.0)
            new = conc + gas_r[b, pl.ds(128 + 8 * j, 8), :] * change
            gas_c[step + 1, b, rows(j), :] = new
            if step == 0:
                gas_f[1, b, rows(j), :] = root * new

    def gas_first(b, carry):
        gas_advance(0, b)
        return carry

    lax.fori_loop(0, 3, gas_first, 0)
    gas_advance(1, 1)

    pack_planes(gas_c[2, 1], send_o, recv_o)
    scatter4(send_o, recv_o, 4)

    def planes(src):
        return jnp.concatenate([src[i] for i in range(NX)], axis=0).T

    most4 = pl.ds(0, NX - 1)
    wait_all(recv_h.at[most4], sems.at[1, 3])
    field = planes(recv_h)
    for j in range(SEG):
        head_out[0, pl.ds(j, SUB, stride=SEG), :] = field[8 * j : 8 * j + 8]

    wait_all(recv_o.at[most4], sems.at[1, 4])
    field = planes(recv_o)
    for j in range(SEG):
        tmp2[pl.ds(j, SUB, stride=SEG), :] = field[8 * j : 8 * j + 8]

    def body_brick(k, c):
        ty = (y + k) % NYD
        remote(
            tmp2.at[pl.ds(pl.multiple_of(16 * ty, 16), 16)],
            brick.at[y],
            sems.at[0, 5],
            sems.at[1, 5],
            (g, ty),
        ).start()
        return c

    lax.fori_loop(1, NYD, body_brick, 0)
    brick[y] = tmp2[pl.ds(pl.multiple_of(16 * y, 16), 16), :]
    wait_all(brick.at[pl.ds(0, NYD - 1)], sems.at[1, 5])
    for i in range(NYD):
        oxy_out[0, :, 128 * i : 128 * i + 128] = brick[i]

    halo(reg_a, 0, 2, (-1, 1, -2, 2), False)
    halo(reg_c, 1, 2, (-1, 1, -2, 2), False)
    halo(reg_d, 2, 1, (-1, 1), False)
    halo(reg_b, 3, 1, (-1, 1), False)
    wait_all(recv_a.at[most8], sems.at[0, 0])
    wait_all(recv_x.at[pl.ds(0, NX - 1)], sems.at[0, 1])
    wait_all(recv_b.at[most8], sems.at[0, 2])
    wait_all(recv_h.at[most4], sems.at[0, 3])
    wait_all(recv_o.at[most4], sems.at[0, 4])
    wait_all(brick.at[pl.ds(0, NYD - 1)], sems.at[0, 5])


def local(pressure_head, material_zone, emitters, oxygen, sulfide_rate, air_flux):
    vmem = pl.BlockSpec(memory_space=pltpu.VMEM)
    f32 = jnp.float32

    def buf(*shape):
        return pltpu.VMEM(shape, f32)

    block = (DEPTH, LANES)
    return pl.pallas_call(
        kernel,
        out_shape=(
            jax.ShapeDtypeStruct((1, DEPTH, LANES), f32),
            jax.ShapeDtypeStruct((1, DEPTH // NYD, LANES * NYD), f32),
        ),
        in_specs=[vmem] * 6,
        out_specs=(vmem, vmem),
        scratch_shapes=[
            buf(*block),
            buf(*block),
            buf(8 * NX, LANES),
            buf(8 * NX, LANES),
            buf(8 * NX, LANES),
            buf(8 * NX, LANES),
            buf(2, LANES),
            buf(NX, 2, LANES),
            buf(REGION, 264, LANES),
            buf(3, 256, LANES),
            buf(REGION, *block),
            buf(3, *block),
            buf(REGION, *block),
            buf(REGION, *block),
            buf(REGION, *block),
            buf(REGION, *block),
            buf(REGION, 5, *block),
            buf(REGION, 8 * NFAC, LANES),
            buf(2, REGION, *block),
            buf(3, *block),
            buf(2, 3, *block),
            buf(3, 3, *block),
            buf(3, 256, LANES),
            buf(NX, COLS, LANES),
            buf(NX, COLS, LANES),
            buf(NX, COLS, LANES),
            buf(NX, COLS, LANES),
            buf(NYD, DEPTH // NYD, LANES),
            pltpu.SemaphoreType.DMA((2, 6)),
            pltpu.SemaphoreType.DMA((4, REGION)),
            pltpu.SemaphoreType.DMA((4, REGION)),
        ],
        compiler_params=pltpu.CompilerParams(
            collective_id=0, has_side_effects=True, vmem_limit_bytes=32 * 1024 * 1024
        ),
    )(pressure_head, material_zone, emitters, oxygen, sulfide_rate, air_flux)


def solution(mesh):
    return jax.shard_map(
        local,
        mesh=mesh,
        in_specs=(
            P("gx", None, "gy"),
            P("gx", None, "gy"),
            P("gx", "gy"),
            P("gx", None, "gy"),
            P("gx", None, "gy"),
            P("gx", "gy"),
        ),
        out_specs=(P("gx", None, "gy"), P("gx", "gy", None)),
        check_vma=False,
    )
```

time: 592 us -> 80.6 us (0.14)
  the two profiles are of different devices: /device:TPU:22 before, /device:TPU:1 now
where the time goes in v1:
time: 80.6 us; the launch traced here: 80.3 us
  Pallas kernels  73.7 us (91%)
  local copies, waits for them, and re-layouts  5.92 us (7%)
    pallas_call x1, Pallas kernels, local(): pl.pallas_call(kernel, out_shape=(jax.ShapeDtypeStruct((1, DEPTH, LANES),...  73.7 us
    unnamed x14, local copies, waits for them, and re-layouts  5.92 us

profile of v1, /device:TPU:1, one launch (start us, length us, event | category | flops | bytes accessed | tf_op | source)
XLA Modules:
  0.0 80.3 jit_solution(17195291515447421633)
XLA Ops:
  0.6 0.0 copy-start
  0.6 0.8 %copy-done = f32[1,128,128]{2,1,0:T(8,128)S(1)} copy-done((f32[1,128,128]{2,1,0:T(8,128)S(1)}, f32[1,128,128]{2,1,0:T(8,128)}, u32[]{:S(2)}) %copy-start) | copy-done | bytes 65560
  1.5 0.0 copy-start.1
  1.5 0.8 %copy-done.1 = s32[1,128,128]{2,1,0:T(8,128)S(1)} copy-done((s32[1,128,128]{2,1,0:T(8,128)S(1)}, s32[1,128,128]{2,1,0:T(8,128)}, u32[]{:S(2)}) %copy-start.1) | copy-done | bytes 65560
  2.3 0.0 copy-start.2
  2.3 0.8 %copy-done.2 = f32[1,128,128]{2,1,0:T(8,128)S(1)} copy-done((f32[1,128,128]{2,1,0:T(8,128)S(1)}, f32[1,128,128]{2,1,0:T(8,128)}, u32[]{:S(2)}) %copy-start.2) | copy-done | bytes 65560
  3.2 0.0 copy-start.3
  3.2 0.8 %copy-done.3 = f32[1,128,128]{2,1,0:T(8,128)S(1)} copy-done((f32[1,128,128]{2,1,0:T(8,128)S(1)}, f32[1,128,128]{2,1,0:T(8,128)}, u32[]{:S(2)}) %copy-start.3) | copy-done | bytes 65560
  4.0 0.0 copy-start.4
  4.0 0.7 copy-done.4
  4.6 0.0 copy-start.5
  4.7 0.7 copy-done.5
  5.3 73.7 %shard_map.77 = (f32[1,128,128]{2,1,0:T(8,128)S(1)}, f32[1,16,1024]{2,1,0:T(8,128)S(1)}) custom-call(f32[1,128,128]{2,1,0:T(8,128)S(1)} %copy-done, s32[1,128,128]{2,1,0:T(8,128)S(1)} %copy-done.1, s32[1,128]{1,0:T(1,128)S(1)} %copy-done.4, f32[1,128,128]{2,1,0:T(8,128)S(1)} %copy-done.2, f32[1,128,128]{2,1,0:T(8,128)S(1)} %copy-done.3, f32[1,128]{1,0:T(1,128)S(1)} %copy-done.5), custom_call_target="tpu_custom_call" | custom-call | tf_op jit(solution)/shard_map/pallas_call | solution.py:579
  79.0 0.6 copy.10
  79.6 0.6 copy.11
Async XLA Ops:
  0.6 0.8 %copy-start = (f32[1,128,128]{2,1,0:T(8,128)S(1)}, f32[1,128,128]{2,1,0:T(8,128)}, u32[]{:S(2)}) copy-start(f32[1,128,128]{2,1,0:T(8,128)} %head_ref.1) | copy-start | bytes 196612
  1.5 0.8 %copy-start.1 = (s32[1,128,128]{2,1,0:T(8,128)S(1)}, s32[1,128,128]{2,1,0:T(8,128)}, u32[]{:S(2)}) copy-start(s32[1,128,128]{2,1,0:T(8,128)} %zone_ref.1) | copy-start | bytes 196612
  2.3 0.8 %copy-start.2 = (f32[1,128,128]{2,1,0:T(8,128)S(1)}, f32[1,128,128]{2,1,0:T(8,128)}, u32[]{:S(2)}) copy-start(f32[1,128,128]{2,1,0:T(8,128)} %oxy_ref.1) | copy-start | bytes 196612
  3.2 0.8 %copy-start.3 = (f32[1,128,128]{2,1,0:T(8,128)S(1)}, f32[1,128,128]{2,1,0:T(8,128)}, u32[]{:S(2)}) copy-start(f32[1,128,128]{2,1,0:T(8,128)} %sul_ref.1) | copy-start | bytes 196612
  4.0 0.7 copy-start.4
  4.6 0.7 copy-start.5

commit v2 on v1

--- a/solution.py
+++ b/solution.py
@@ -29,7 +29,8 @@
 BACK = 30
 SCALE = 60
 LAST = 67
-NFAC = 74
+PREV = 75
+NFAC = 83
 
 
 def levels():
@@ -94,9 +95,10 @@
     head_ref, zone_ref, em_ref, oxy_ref, sul_ref, flux_ref,
     head_out, oxy_out,
     tmp, tmp2, send_a, recv_a, send_b, recv_b, send_x, recv_x, reg_a, reg_b, reg_c, reg_d,
-    cond, half_cap, se_old, base, lat, fac, x, gas_g, gas_f, gas_c, gas_r,
-    send_h, recv_h, send_o, recv_o, brick,
-    sems, halo_s, halo_r,
+    cond, half_cap, se_old, raw, base, lat, face, row_a, row_c, fac, x, f,
+    gas_g, gas_s, gas_f0, gas_f1, gas_c, gas_r,
+    send_h, recv_h, send_o, recv_o, brick, in_h, in_z, in_o, in_s, in_e, in_f,
+    sems, halo_s, halo_r, in_sem,
 ):
     g = lax.axis_index("gx")
     y = lax.axis_index("gy")
@@ -131,12 +133,23 @@
     def valid(k):
         return jnp.logical_and(me + k >= 0, me + k < STRIPS)
 
-    lax.fori_loop(1, NX, greet_x, 0)
-    lax.fori_loop(1, NYD, greet_y, 0)
+    lax.fori_loop(1, NX, greet_x, 0, unroll=True)
+    lax.fori_loop(1, NYD, greet_y, 0, unroll=True)
     for k in (-1, 1, -2, 2):
         @pl.when(jnp.logical_and(valid(k), jnp.logical_or(s + k < 0, s + k >= NX)))
         def _():
             pl.semaphore_signal(barrier, inc=1, device_id=device_of(me + k), device_id_type=MESH)
+
+    loads = [
+        pltpu.make_async_copy(src.at[0], dst, in_sem.at[i])
+        for i, (src, dst) in enumerate(
+            ((head_ref, in_h), (zone_ref, in_z), (oxy_ref, in_o), (sul_ref, in_s))
+        )
+    ]
+    loads.append(pltpu.make_async_copy(em_ref, in_e, in_sem.at[4]))
+    loads.append(pltpu.make_async_copy(flux_ref, in_f, in_sem.at[5]))
+    for load in loads:
+        load.start()
 
     def pack(first, second, out):
         for q in range(NX // 2):
@@ -147,12 +160,16 @@
 
     def segmented(ref):
         return jnp.concatenate(
-            [ref[0, pl.ds(j, SUB, stride=SEG), :].astype(jnp.float32) for j in range(SEG)], axis=0
+            [ref[pl.ds(j, SUB, stride=SEG), :].astype(jnp.float32) for j in range(SEG)], axis=0
         ).T
 
-    pack(segmented(head_ref), segmented(zone_ref), send_a)
-    send_x[0:1, :] = em_ref[...].astype(jnp.float32)
-    send_x[1:2, :] = flux_ref[...]
+    loads[0].wait()
+    loads[1].wait()
+    pack(segmented(in_h), segmented(in_z), send_a)
+    loads[4].wait()
+    loads[5].wait()
+    send_x[0:1, :] = in_e[...].astype(jnp.float32)
+    send_x[1:2, :] = in_f[...]
     own = pl.ds(pl.multiple_of(8 * g, 8), 8)
     recv_a[own, :] = send_a[pl.ds(pl.multiple_of(8 * s, 8), 8), :]
     recv_x[g] = send_x[...]
@@ -192,7 +209,9 @@
 
     lax.fori_loop(1, NX, body_x, 0)
 
-    pack(segmented(oxy_ref), segmented(sul_ref), send_b)
+    loads[2].wait()
+    loads[3].wait()
+    pack(segmented(in_o), segmented(in_s), send_b)
     recv_b[own, :] = send_b[pl.ds(pl.multiple_of(8 * s, 8), 8), :]
 
     most8 = pl.ds(0, 8 * (NX - 1))
@@ -280,148 +299,218 @@
                 rest = 1.0 - filled
                 cond[b, rows(j), :] = sel(masks, kk) * (jnp.exp2(-0.5 * mlog) * rest * rest + COND_FLOOR)
                 half_cap[b, rows(j), :] = cap
-                x[0, b, rows(j), :] = h
+                x[b, rows(j), :] = h
                 if first:
                     se_old[b, rows(j), :] = se
-                    base[b, rows(j), :] = cap * h
+                    raw[b, rows(j), :] = cap * h
                 else:
-                    base[b, rows(j), :] = cap * h - sel(
+                    raw[b, rows(j), :] = cap * h - sel(
                         masks, [(w - v) / FLOW_STEP for v, w in zip(r, sat)]
                     ) * (se - se_old[b, rows(j), :])
             return carry
 
         lax.fori_loop(0, REGION, retain, 0)
 
-        def assemble(b, carry):
-            after, before = jnp.minimum(b + 1, REGION - 1), jnp.maximum(b - 1, 0)
+        def right_faces(b, carry):
+            after = jnp.minimum(b + 1, REGION - 1)
             strip = me + b - 2
             closed = jnp.logical_or(strip == -1, strip == STRIPS - 1)
-            open_face = jnp.where(closed, 0.0, 1.0)
-            right_mask = jnp.where(last_col, open_face, 1.0)
+            mask = jnp.where(last_col, jnp.where(closed, 0.0, 1.0), 1.0)
+            for j in range(SEG):
+                k = cond[b, rows(j), :]
+                near = roll(jnp.where(first_col, cond[after, rows(j), :], k), -NX, 1)
+                face[b, rows(j), :] = mask * harmonic(k, near)
+            return carry
+
+        lax.fori_loop(0, REGION, right_faces, 0)
+
+        def assemble(b, carry):
+            before = jnp.maximum(b - 1, 0)
             ks = [cond[b, rows(j), :] for j in range(SEG)]
-            ups = [harmonic(ks[j], ks[j - 1]) for j in range(1, SEG)]
             up0 = jnp.where(top, 0.0, harmonic(ks[0], roll(ks[SEG - 1], 1, 0)))
-            ups = [up0] + ups
+            ups = [up0] + [harmonic(ks[j], ks[j - 1]) for j in range(1, SEG)]
             los = ups[1:] + [roll(up0, -1, 0)]
-            av, cv = [], []
             for j in range(SEG):
                 k = ks[j]
                 xp = jnp.where(last_plane, 0.0, harmonic(k, roll(k, -1, 1)))
                 xm = roll(xp, 1, 1)
-                yp = right_mask * harmonic(
-                    k, roll(jnp.where(first_col, cond[after, rows(j), :], k), -NX, 1)
-                )
-                lat[b, 3, rows(j), :] = yp
-                ym = roll(jnp.where(last_col, lat[before, 3, rows(j), :], yp), NX, 1)
+                yp = face[b, rows(j), :]
+                ym = roll(jnp.where(last_col, face[before, rows(j), :], yp), NX, 1)
                 diag = half_cap[b, rows(j), :] + xp + xm + yp + ym + ups[j] + los[j]
                 inv = 1.0 / diag
-                rhs = base[b, rows(j), :] + ups[j] - los[j]
+                rhs = raw[b, rows(j), :] + ups[j] - los[j]
                 if j == SEG - 1:
                     rhs = rhs - jnp.where(bottom, k, 0.0)
                 if j == 0:
                     rhs = rhs + jnp.where(top, IRRIGATION * reg_a[b, pl.ds(256, 1), :], 0.0)
                 base[b, rows(j), :] = rhs * inv
-                lat[b, 0, rows(j), :] = xm * inv
-                lat[b, 1, rows(j), :] = xp * inv
-                lat[b, 2, rows(j), :] = ym * inv
-                lat[b, 4, rows(j), :] = yp * inv
-                av.append(ups[j] * inv)
-                cv.append(los[j] * inv)
-
-            def put(i, value):
+                lat[b, rows(j), :] = xm * inv
+                lat[b, rows(SEG + j), :] = xp * inv
+                lat[b, rows(2 * SEG + j), :] = ym * inv
+                lat[b, rows(3 * SEG + j), :] = yp * inv
+                row_a[b, rows(j), :] = ups[j] * inv
+                row_c[b, rows(j), :] = los[j] * inv
+            return carry
+
+        lax.fori_loop(0, REGION, assemble, 0)
+
+        def factor(blocks):
+            state = {}
+            for b in blocks:
+                state[b] = (
+                    [row_a[b, rows(j), :] for j in range(SEG)],
+                    [None] * SEG,
+                    [row_c[b, rows(j), :] for j in range(SEG)],
+                )
+
+            def put(b, i, value):
                 fac[b, rows(i), :] = value
 
-            bv = [None] * SEG
             for step, gone, stay, place, scale in LEVELS:
-                for i, e in enumerate(gone):
-                    if step > 1:
-                        rec = 1.0 / bv[e]
-                        put(SCALE + scale + i, rec)
-                        av[e] = av[e] * rec
-                        cv[e] = cv[e] * rec
-                        bv[e] = rec
-                    put(BACK + place + i, av[e])
-                    put(BACK + 15 + place + i, cv[e])
-                new = {}
-                for i, j in enumerate(stay):
-                    up, dn = j - step, j + step
-                    if dn < SEG:
+                for b in blocks:
+                    av, bv, cv = state[b]
+                    for i, e in enumerate(gone):
+                        if step > 1:
+                            bv[e] = 1.0 / bv[e]
+                            put(b, SCALE + scale + i, bv[e])
+                            av[e] = av[e] * bv[e]
+                            cv[e] = cv[e] * bv[e]
+                        put(b, BACK + place + i, av[e])
+                        put(b, BACK + 15 + place + i, cv[e])
+                for b in blocks:
+                    av, bv, cv = state[b]
+                    new = {}
+                    for i, j in enumerate(stay):
+                        up, dn = j - step, j + step
+                        wrap = dn >= SEG
+                        dn = dn % SEG
                         a_dn, c_dn = av[dn], cv[dn]
-                        r_dn = bv[dn] if step > 1 else None
+                        alpha, gamma = av[j], cv[j]
+                        if step > 1:
+                            alpha = alpha * bv[up]
+                        if wrap:
+                            a_dn, c_dn = roll(a_dn, -1, 0), roll(c_dn, -1, 0)
+                            gamma = roll(gamma, 1, 0)
+                        if step > 1:
+                            gamma = gamma * bv[dn]
+                        diag = (bv[j] if step > 1 else 1.0) - av[j] * cv[up] - cv[j] * a_dn
+                        put(b, FWD + place + i, alpha)
+                        put(b, FWD + 15 + place + i, gamma)
+                        new[j] = (av[j] * av[up], diag, cv[j] * c_dn)
+                    for j in stay:
+                        av[j], bv[j], cv[j] = new[j]
+            last = {b: (v[0][SEG - 1], v[1][SEG - 1], v[2][SEG - 1]) for b, v in state.items()}
+            multipliers = {b: [] for b in blocks}
+            for step in (1, 2, 4):
+                for b in blocks:
+                    a, d, c = last[b]
+                    inv = 1.0 / d
+                    alpha = a * roll(inv, step, 0)
+                    gamma = c * roll(inv, -step, 0)
+                    multipliers[b].append((alpha, gamma))
+                    d = d - alpha * roll(c, step, 0) - gamma * roll(a, -step, 0)
+                    last[b] = (alpha * roll(a, step, 0), d, gamma * roll(c, -step, 0))
+            for b in blocks:
+                (a1, g1), (a2, g2), (a4, g4) = multipliers[b]
+                beta = a4 + g4
+                inv = 1.0 / last[b][1]
+                diags = [
+                    None,
+                    a1 + a2 * roll(g1, 2, 0),
+                    a2,
+                    a2 * roll(a1, 2, 0),
+                    None,
+                    g2 * roll(g1, -2, 0),
+                    g2,
+                    g1 + g2 * roll(a1, -2, 0),
+                ]
+                final = []
+                for k in range(SUB):
+                    if k == 0:
+                        value = inv
+                    elif k == 4:
+                        value = inv * beta
                     else:
-                        a_dn, c_dn = roll(av[dn - SEG], -1, 0), roll(cv[dn - SEG], -1, 0)
-                        r_dn = roll(bv[dn - SEG], -1, 0) if step > 1 else None
-                    diag = (bv[j] if step > 1 else 1.0) - av[j] * cv[up] - cv[j] * a_dn
-                    alpha = av[j] * bv[up] if step > 1 else av[j]
-                    gamma = cv[j] * r_dn if step > 1 else cv[j]
-                    put(FWD + place + i, alpha)
-                    put(FWD + 15 + place + i, gamma)
-                    new[j] = (av[j] * av[up], diag, cv[j] * c_dn)
-                for j in stay:
-                    av[j], bv[j], cv[j] = new[j]
-            a, d, c = av[SEG - 1], bv[SEG - 1], cv[SEG - 1]
-            for i, step in enumerate((1, 2, 4)):
-                alpha = a / roll(d, step, 0)
-                gamma = c / roll(d, -step, 0)
-                put(LAST + 2 * i, alpha)
-                put(LAST + 2 * i + 1, gamma)
-                d = d - alpha * roll(c, step, 0) - gamma * roll(a, -step, 0)
-                a, c = alpha * roll(a, step, 0), gamma * roll(c, -step, 0)
-            put(LAST + 6, 1.0 / d)
-            return carry
-
-        lax.fori_loop(0, REGION, assemble, 0)
-
-        def relax(now, b):
-            def get(i):
+                        value = inv * (diags[k] + beta * roll(diags[(k + 4) % 8], 4, 0))
+                    put(b, LAST + k, value)
+                    put(b, PREV + (k + 1) % 8, roll(value, 1, 0))
+
+        factor((0, 1, 2))
+        factor((3, 4))
+
+        def sources(b):
+            before, after = max(b - 1, 0), min(b + 1, REGION - 1)
+            for j in range(SEG):
+                v = x[b, rows(j), :]
+                left = jnp.where(last_col, x[before, rows(j), :], v)
+                right = jnp.where(first_col, x[after, rows(j), :], v)
+                f[b, rows(j), :] = (
+                    base[b, rows(j), :]
+                    + lat[b, rows(j), :] * roll(v, 1, 1)
+                    + lat[b, rows(SEG + j), :] * roll(v, -1, 1)
+                    + lat[b, rows(2 * SEG + j), :] * roll(left, NX, 1)
+                    + lat[b, rows(3 * SEG + j), :] * roll(right, -NX, 1)
+                )
+
+        def solve(blocks):
+            def get(b, i):
                 return fac[b, rows(i), :]
 
-            later = 1 - now
-            f = []
-            for j in range(SEG):
-                v = x[now, b, rows(j), :]
-                left = jnp.where(last_col, x[now, max(b - 1, 0), rows(j), :], v)
-                right = jnp.where(first_col, x[now, min(b + 1, REGION - 1), rows(j), :], v)
-                f.append(
-                    base[b, rows(j), :]
-                    + lat[b, 0, rows(j), :] * roll(v, 1, 1)
-                    + lat[b, 1, rows(j), :] * roll(v, -1, 1)
-                    + lat[b, 2, rows(j), :] * roll(left, NX, 1)
-                    + lat[b, 4, rows(j), :] * roll(right, -NX, 1)
-                )
+            values = {b: [f[b, rows(j), :] for j in range(SEG)] for b in blocks}
+            wrapped = {b: None for b in blocks}
             for step, gone, stay, place, scale in LEVELS:
-                for i, j in enumerate(stay):
-                    dn = f[j + step] if j + step < SEG else roll(f[j + step - SEG], -1, 0)
-                    f[j] = f[j] + get(FWD + place + i) * f[j - step] + get(FWD + 15 + place + i) * dn
-            v = f[SEG - 1]
-            for i, step in enumerate((1, 2, 4)):
-                v = v + get(LAST + 2 * i) * roll(v, step, 0) + get(LAST + 2 * i + 1) * roll(v, -step, 0)
-            f[SEG - 1] = v * get(LAST + 6)
-            wrapped = roll(f[SEG - 1], 1, 0)
+                for b in blocks:
+                    v = values[b]
+                    for i, j in enumerate(stay):
+                        v[j] = v[j] + get(b, FWD + place + i) * v[j - step]
+                        gamma = get(b, FWD + 15 + place + i)
+                        if j + step < SEG:
+                            v[j] = v[j] + gamma * v[j + step]
+                        elif step == 1:
+                            wrapped[b] = gamma * v[0]
+                        else:
+                            wrapped[b] = wrapped[b] + gamma * v[j + step - SEG]
+            lasts = {}
+            for b in blocks:
+                lasts[b] = values[b][SEG - 1] + roll(wrapped[b], -1, 0)
+            above = {}
+            for b in blocks:
+                turned = [lasts[b]] + [roll(lasts[b], k, 0) for k in range(1, SUB)]
+                here = [get(b, LAST + k) * turned[k] for k in range(SUB)]
+                prev = [get(b, PREV + k) * turned[k] for k in range(SUB)]
+                while len(here) > 1:
+                    here = [p + q for p, q in zip(here[0::2], here[1::2])]
+                    prev = [p + q for p, q in zip(prev[0::2], prev[1::2])]
+                values[b][SEG - 1] = here[0]
+                above[b] = prev[0]
             for step, gone, stay, place, scale in reversed(LEVELS):
-                for i, e in enumerate(gone):
-                    up = f[e - step] if e >= step else wrapped
-                    src = f[e] * get(SCALE + scale + i) if step > 1 else f[e]
-                    f[e] = src + get(BACK + place + i) * up + get(BACK + 15 + place + i) * f[e + step]
-            for j in range(SEG):
-                x[later, b, rows(j), :] = f[j]
-
-        def wide(t, carry):
-            for b in range(REGION):
-                relax(t % 2, b)
-            return carry
-
-        def narrow(t, carry):
-            for b in (1, 2, 3):
-                relax(t % 2, b)
-            return carry
-
-        lax.fori_loop(0, 3, wide, 0)
-        lax.fori_loop(3, 7, narrow, 0)
-        relax(1, 2)
+                for b in blocks:
+                    v = values[b]
+                    for i, e in enumerate(gone):
+                        up = v[e - step] if e >= step else above[b]
+                        src = v[e] * get(b, SCALE + scale + i) if step > 1 else v[e]
+                        v[e] = src + get(b, BACK + place + i) * up + get(b, BACK + 15 + place + i) * v[e + step]
+            for b in blocks:
+                for j in range(SEG):
+                    x[b, rows(j), :] = values[b][j]
+
+        def relax(groups):
+            def body(t, carry):
+                for group in groups:
+                    for b in group:
+                        sources(b)
+                for group in groups:
+                    solve(group)
+                return carry
+
+            return body
+
+        lax.fori_loop(0, 3, relax(((0, 1, 2), (3, 4))), 0)
+        lax.fori_loop(3, 7, relax(((1, 2, 3),)), 0)
+        relax(((2,),))(7, 0)
 
     picard(reg_a, 0, True)
-    reg_c[2] = x[0, 2]
+    reg_c[2] = x[2]
     halo(reg_c, 1, 2, (-1, 1, -2, 2), True)
 
     wait_all(recv_b.at[most8], sems.at[1, 2])
@@ -430,7 +519,7 @@
     halo(reg_b, 3, 1, (-1, 1), True)
 
     picard(reg_c, 1, False)
-    reg_d[1] = x[0, 2]
+    reg_d[1] = x[2]
     halo(reg_d, 2, 1, (-1, 1), True)
 
     def scatter4(src, dst, index):
@@ -447,7 +536,7 @@
             out[p] = tmp[pl.ds(p, COLS, stride=NX), :]
         own_slot[s] = out[g]
 
-    pack_planes(x[0, 2], send_h, recv_h)
+    pack_planes(x[2], send_h, recv_h)
     scatter4(send_h, recv_h, 3)
 
     def gas_prepare(i, carry):
@@ -471,58 +560,63 @@
             root = jnp.exp2((5.0 / 3.0) * jnp.log2(gas)) * inv_s * inside
             conc = reg_b[b, rows(j), :]
             gas_g[b, rows(j), :] = root
-            gas_f[0, b, rows(j), :] = root * conc
-            gas_c[0, b, rows(j), :] = conc
+            gas_f0[b, rows(j), :] = root * conc
             gas_r[b, rows(j), :] = reg_b[b, pl.ds(128 + 8 * j, 8), :] * (sel(masks, r) + span * se) * inv_s
             gas_r[b, pl.ds(128 + 8 * j, 8), :] = GAS_STEP * inv_s
         return carry
 
     lax.fori_loop(0, 3, gas_prepare, 0)
 
-    def gas_advance(step, b):
-        before, after = jnp.maximum(b - 1, 0), jnp.minimum(b + 1, 2)
-
-        def total(get, j):
-            v = get(b, j)
-            left = jnp.where(last_col, get(before, j), v)
-            right = jnp.where(first_col, get(after, j), v)
-            above = get(b, j - 1) if j > 0 else jnp.where(top, 0.0, roll(get(b, SEG - 1), 1, 0))
-            below = get(b, j + 1) if j < SEG - 1 else jnp.where(bottom, 0.0, roll(get(b, 0), -1, 0))
-            return (
-                jnp.where(first_plane, 0.0, roll(v, 1, 1))
-                + jnp.where(last_plane, 0.0, roll(v, -1, 1))
-                + roll(left, NX, 1)
-                + roll(right, -NX, 1)
-                + above
-                + below
-            )
-
+    def around(ref, b, j):
+        before, after = max(b - 1, 0), min(b + 1, 2)
+        v = ref[b, rows(j), :]
+        left = jnp.where(last_col, ref[before, rows(j), :], v)
+        right = jnp.where(first_col, ref[after, rows(j), :], v)
+        above = ref[b, rows(j - 1), :] if j > 0 else jnp.where(top, 0.0, roll(ref[b, rows(SEG - 1), :], 1, 0))
+        below = ref[b, rows(j + 1), :] if j < SEG - 1 else jnp.where(bottom, 0.0, roll(ref[b, rows(0), :], -1, 0))
+        return (
+            jnp.where(first_plane, 0.0, roll(v, 1, 1))
+            + jnp.where(last_plane, 0.0, roll(v, -1, 1))
+            + roll(left, NX, 1)
+            + roll(right, -NX, 1)
+            + above
+            + below
+        )
+
+    def gas_advance(b, old, flow, store):
         flux = reg_a[b + 1, pl.ds(257, 1), :]
         for j in range(SEG):
-            conc = gas_c[step, b, rows(j), :]
+            conc = old[b, rows(j), :]
             root = gas_g[b, rows(j), :]
-            sum_f = total(lambda bb, jj: gas_f[step, bb, rows(jj), :], j)
-            sum_g = total(lambda bb, jj: gas_g[bb, rows(jj), :], j)
             if j < SEG - 1:
-                under = gas_c[step, b, rows(j + 1), :]
+                under = old[b, rows(j + 1), :]
             else:
-                under = jnp.where(bottom, 1.0, roll(gas_c[step, b, rows(0), :], -1, 0))
-            change = root * (sum_f - conc * sum_g) + flux * (under - conc) - gas_r[b, rows(j), :] * conc
+                under = jnp.where(bottom, 1.0, roll(old[b, rows(0), :], -1, 0))
+            change = (
+                root * (around(flow, b, j) - conc * gas_s[b, rows(j), :])
+                + flux * (under - conc)
+                - gas_r[b, rows(j), :] * conc
+            )
             if j == 0:
                 change = change + jnp.where(top, 2.0 * root * root * (1.0 - conc), 0.0)
-            new = conc + gas_r[b, pl.ds(128 + 8 * j, 8), :] * change
-            gas_c[step + 1, b, rows(j), :] = new
-            if step == 0:
-                gas_f[1, b, rows(j), :] = root * new
-
-    def gas_first(b, carry):
-        gas_advance(0, b)
-        return carry
-
-    lax.fori_loop(0, 3, gas_first, 0)
-    gas_advance(1, 1)
-
-    pack_planes(gas_c[2, 1], send_o, recv_o)
+            store(j, conc + gas_r[b, pl.ds(128 + 8 * j, 8), :] * change, root)
+
+    for b in range(3):
+
+        def first_store(j, new, root, b=b):
+            gas_c[b, rows(j), :] = new
+            gas_f1[b, rows(j), :] = root * new
+
+        for j in range(SEG):
+            gas_s[b, rows(j), :] = around(gas_g, b, j)
+        gas_advance(b, reg_b, gas_f0, first_store)
+
+    def second_store(j, new, root):
+        tmp2[rows(j), :] = new
+
+    gas_advance(1, gas_c, gas_f1, second_store)
+
+    pack_planes(tmp2[...], send_o, recv_o)
     scatter4(send_o, recv_o, 4)
 
     def planes(src):
@@ -576,13 +670,13 @@
         return pltpu.VMEM(shape, f32)
 
     block = (DEPTH, LANES)
-    return pl.pallas_call(
+    done = pl.pallas_call(
         kernel,
         out_shape=(
             jax.ShapeDtypeStruct((1, DEPTH, LANES), f32),
             jax.ShapeDtypeStruct((1, DEPTH // NYD, LANES * NYD), f32),
         ),
-        in_specs=[vmem] * 6,
+        in_specs=[pl.BlockSpec(memory_space=pl.ANY)] * 6,
         out_specs=(vmem, vmem),
         scratch_shapes=[
             buf(*block),
@@ -601,26 +695,51 @@
             buf(REGION, *block),
             buf(REGION, *block),
             buf(REGION, *block),
-            buf(REGION, 5, *block),
+            buf(REGION, *block),
+            buf(REGION, 4 * DEPTH, LANES),
+            buf(REGION, *block),
+            buf(REGION, *block),
+            buf(REGION, *block),
             buf(REGION, 8 * NFAC, LANES),
-            buf(2, REGION, *block),
+            buf(REGION, *block),
+            buf(REGION, *block),
             buf(3, *block),
-            buf(2, 3, *block),
-            buf(3, 3, *block),
+            buf(3, *block),
+            buf(3, *block),
+            buf(3, *block),
+            buf(3, *block),
             buf(3, 256, LANES),
             buf(NX, COLS, LANES),
             buf(NX, COLS, LANES),
             buf(NX, COLS, LANES),
             buf(NX, COLS, LANES),
             buf(NYD, DEPTH // NYD, LANES),
+            buf(*block),
+            pltpu.VMEM(block, jnp.int32),
+            buf(*block),
+            buf(*block),
+            pltpu.VMEM((1, LANES), jnp.int32),
+            buf(1, LANES),
             pltpu.SemaphoreType.DMA((2, 6)),
             pltpu.SemaphoreType.DMA((4, REGION)),
             pltpu.SemaphoreType.DMA((4, REGION)),
+            pltpu.SemaphoreType.DMA((6,)),
         ],
         compiler_params=pltpu.CompilerParams(
-            collective_id=0, has_side_effects=True, vmem_limit_bytes=32 * 1024 * 1024
+            collective_id=0, has_side_effects=True, vmem_limit_bytes=64 * 1024 * 1024
         ),
     )(pressure_head, material_zone, emitters, oxygen, sulfide_rate, air_flux)
+    return pl.pallas_call(
+        finish,
+        out_shape=tuple(jax.ShapeDtypeStruct(v.shape, f32) for v in done),
+        in_specs=[vmem] * 2,
+        out_specs=(vmem, vmem),
+    )(*done)
+
+
+def finish(head, oxygen, head_out, oxygen_out):
+    head_out[...] = head[...]
+    oxygen_out[...] = oxygen[...]
 
 
 def solution(mesh):

time: 80.6 us -> 58.8 us (0.73)
  Pallas kernels: 73.7 us -> 57.9 us
  local copies, waits for them, and re-layouts: 5.92 us -> 0 us
    pallas_call x1, Pallas kernels: 73.7 us -> 56.4 us  [local(): pl.pallas_call(kernel, out_shape=(jax.ShapeDtypeStruct((1, DEPTH, LANES),...]
    unnamed x14 -> x0, local copies, waits for them, and re-layouts: 5.92 us -> none
    pallas_call x0 -> x1, Pallas kernels: none -> 1.53 us  [local(): pl.pallas_call(finish, out_shape=tuple((jax.ShapeDtypeStruct(v.shape, f32...]
where the time goes in v2:
time: 58.8 us; the launch traced here: 58.6 us
  Pallas kernels  57.9 us (98%)
  between operations  0.64 us (1%)
    pallas_call x1, Pallas kernels, local(): pl.pallas_call(kernel, out_shape=(jax.ShapeDtypeStruct((1, DEPTH, LANES),...  56.4 us
    pallas_call x1, Pallas kernels, local(): pl.pallas_call(finish, out_shape=tuple((jax.ShapeDtypeStruct(v.shape, f32...  1.53 us

profile of v2, /device:TPU:1, one launch (start us, length us, event | category | flops | bytes accessed | tf_op | source)
XLA Modules:
  0.0 58.6 jit_solution(16127702522489922560)
XLA Ops:
  0.6 56.4 %shard_map.77 = (f32[1,128,128]{2,1,0:T(8,128)}, f32[1,16,1024]{2,1,0:T(8,128)}) custom-call(f32[1,128,128]{2,1,0:T(8,128)} %head_ref.1, s32[1,128,128]{2,1,0:T(8,128)} %zone_ref.1, s32[1,128]{1,0:T(1,128)} %em_ref.1, f32[1,128,128]{2,1,0:T(8,128)} %oxy_ref.1, f32[1,128,128]{2,1,0:T(8,128)} %sul_ref.1, f32[1,128]{1,0:T(1,128)} %flux_ref.1), custom_call_target="tpu_custom_call" | custom-call | tf_op jit(solution)/shard_map/pallas_call | solution.py:673
  57.1 1.5 %shard_map.78 = (f32[1,128,128]{2,1,0:T(8,128)}, f32[1,16,1024]{2,1,0:T(8,128)}) custom-call(f32[1,128,128]{2,1,0:T(8,128)} %get-tuple-element.4.head, f32[1,16,1024]{2,1,0:T(8,128)} %get-tuple-element.5.oxygen), custom_call_target="tpu_custom_call" | custom-call | tf_op jit(solution)/shard_map/pallas_call | solution.py:732

commit v3 on v2

--- a/solution.py
+++ b/solution.py
@@ -94,7 +94,7 @@
 def kernel(
     head_ref, zone_ref, em_ref, oxy_ref, sul_ref, flux_ref,
     head_out, oxy_out,
-    tmp, tmp2, send_a, recv_a, send_b, recv_b, send_x, recv_x, reg_a, reg_b, reg_c, reg_d,
+    tmp, tmp2, send_a, recv_a, send_b, recv_b, send_x, recv_x, reg_a, reg_x, reg_b, reg_c, reg_d,
     cond, half_cap, se_old, raw, base, lat, face, row_a, row_c, fac, x, f,
     gas_g, gas_s, gas_f0, gas_f1, gas_c, gas_r,
     send_h, recv_h, send_o, recv_o, brick, in_h, in_z, in_o, in_s, in_e, in_f,
@@ -120,11 +120,17 @@
     first_col, last_col = col == 0, col == COLS - 1
     top, bottom = sub == 0, sub == SUB - 1
 
+    half, ring, core = g // 16, (g // 2) % 8, g % 2
+    partners = [
+        ((half + dh) % 2) * 16 + ((ring + dz) % 8) * 2 + (core + dc) % 2
+        for dh, dz, dc in sorted(
+            ((dh, dz, dc) for dh in range(2) for dz in range(8) for dc in range(2)),
+            key=lambda d: (-(2 * d[0] + min(d[1], 8 - d[1])), d),
+        )
+        if (dh, dz, dc) != (0, 0, 0)
+    ]
+
     barrier = pltpu.get_barrier_semaphore()
-
-    def greet_x(k, c):
-        pl.semaphore_signal(barrier, inc=1, device_id=((g + k) % NX, y), device_id_type=MESH)
-        return c
 
     def greet_y(k, c):
         pl.semaphore_signal(barrier, inc=1, device_id=(g, (y + k) % NYD), device_id_type=MESH)
@@ -133,7 +139,8 @@
     def valid(k):
         return jnp.logical_and(me + k >= 0, me + k < STRIPS)
 
-    lax.fori_loop(1, NX, greet_x, 0, unroll=True)
+    for tg in partners:
+        pl.semaphore_signal(barrier, inc=1, device_id=(tg, y), device_id_type=MESH)
     lax.fori_loop(1, NYD, greet_y, 0, unroll=True)
     for k in (-1, 1, -2, 2):
         @pl.when(jnp.logical_and(valid(k), jnp.logical_or(s + k < 0, s + k >= NX)))
@@ -184,8 +191,7 @@
         )
 
     def scatter8(src, dst, index):
-        def body(k, c):
-            tg = (g + k) % NX
+        for tg in partners:
             remote(
                 src.at[pl.ds(pl.multiple_of(8 * strip_of(tg), 8), 8)],
                 dst.at[pl.ds(pl.multiple_of(8 * g, 8), 8)],
@@ -193,21 +199,14 @@
                 sems.at[1, index],
                 (tg, y),
             ).start()
-            return c
-
-        lax.fori_loop(1, NX, body, 0)
 
     def wait_all(part, sem):
         pltpu.make_async_copy(part, part, sem).wait()
 
     scatter8(send_a, recv_a, 0)
 
-    def body_x(k, c):
-        tg = (g + k) % NX
+    for tg in partners:
         remote(send_x, recv_x.at[g], sems.at[0, 1], sems.at[1, 1], (tg, y)).start()
-        return c
-
-    lax.fori_loop(1, NX, body_x, 0)
 
     loads[2].wait()
     loads[3].wait()
@@ -225,22 +224,6 @@
 
     reg_a[2, 0:128, :] = unpack(recv_a, 0)
     reg_a[2, 128:256, :] = unpack(recv_a, 1)
-    wait_all(recv_x.at[pl.ds(0, NX - 1)], sems.at[1, 1])
-    tmp[0:32, :] = recv_x[:, 0, :]
-    tmp[32:64, :] = recv_x[:, 1, :]
-    tmp[64:128, :] = jnp.zeros((64, LANES), jnp.float32)
-    tmp2[...] = tmp[...].T
-    emitted = jnp.zeros((1, LANES), jnp.float32)
-    fluxes = jnp.zeros((1, LANES), jnp.float32)
-    lane1 = lax.broadcasted_iota(jnp.int32, (1, LANES), 1) // NX
-    for c in range(COLS):
-        row = tmp2[pl.ds(4 * s + c, 1), :]
-        emitted = jnp.where(lane1 == c, roll(row, 32 * c, 1), emitted)
-        fluxes = jnp.where(lane1 == c, roll(row, 32 * c - 32, 1), fluxes)
-    reg_a[2, 256:264, :] = jnp.concatenate(
-        [emitted, fluxes, jnp.zeros((6, LANES), jnp.float32)], axis=0
-    )
-
     def halo(reg, index, middle, ks, start):
         for k in ks:
             there = middle - k
@@ -272,9 +255,25 @@
             reg[b] = reg[middle]
 
     halo(reg_a, 0, 2, (-1, 1, -2, 2), True)
-    scatter8(send_b, recv_b, 2)
-
-    def picard(reg, index, first):
+    wait_all(recv_x.at[pl.ds(0, NX - 1)], sems.at[1, 1])
+    tmp[0:32, :] = recv_x[:, 0, :]
+    tmp[32:64, :] = recv_x[:, 1, :]
+    tmp[64:128, :] = jnp.zeros((64, LANES), jnp.float32)
+    tmp2[...] = tmp[...].T
+    emitted = jnp.zeros((1, LANES), jnp.float32)
+    fluxes = jnp.zeros((1, LANES), jnp.float32)
+    lane1 = lax.broadcasted_iota(jnp.int32, (1, LANES), 1) // NX
+    for c in range(COLS):
+        row = tmp2[pl.ds(4 * s + c, 1), :]
+        emitted = jnp.where(lane1 == c, roll(row, 32 * c, 1), emitted)
+        fluxes = jnp.where(lane1 == c, roll(row, 32 * c - 32, 1), fluxes)
+    reg_x[2] = jnp.concatenate(
+        [emitted, fluxes, jnp.zeros((6, LANES), jnp.float32)], axis=0
+    )
+
+    halo(reg_x, 4, 2, (-1, 1, -2, 2), True)
+
+    def picard(reg, index, first, meanwhile):
         def retain(i, carry):
             step = (i + 1) // 2
             b = 2 + step * (1 - 2 * (i % 2))
@@ -310,6 +309,7 @@
             return carry
 
         lax.fori_loop(0, REGION, retain, 0)
+        meanwhile()
 
         def right_faces(b, carry):
             after = jnp.minimum(b + 1, REGION - 1)
@@ -342,7 +342,7 @@
                 if j == SEG - 1:
                     rhs = rhs - jnp.where(bottom, k, 0.0)
                 if j == 0:
-                    rhs = rhs + jnp.where(top, IRRIGATION * reg_a[b, pl.ds(256, 1), :], 0.0)
+                    rhs = rhs + jnp.where(top, IRRIGATION * reg_x[b, pl.ds(0, 1), :], 0.0)
                 base[b, rows(j), :] = rhs * inv
                 lat[b, rows(j), :] = xm * inv
                 lat[b, rows(SEG + j), :] = xp * inv
@@ -509,26 +509,26 @@
         lax.fori_loop(3, 7, relax(((1, 2, 3),)), 0)
         relax(((2,),))(7, 0)
 
-    picard(reg_a, 0, True)
+    def start_gas():
+        scatter8(send_b, recv_b, 2)
+        for b in (0, 1, 3, 4):
+            arrive(reg_x, 4, 2, b)
+
+    picard(reg_a, 0, True, start_gas)
     reg_c[2] = x[2]
     halo(reg_c, 1, 2, (-1, 1, -2, 2), True)
 
     wait_all(recv_b.at[most8], sems.at[1, 2])
     reg_b[1, 0:128, :] = unpack(recv_b, 0)
     reg_b[1, 128:256, :] = unpack(recv_b, 1)
-    halo(reg_b, 3, 1, (-1, 1), True)
-
-    picard(reg_c, 1, False)
+
+    picard(reg_c, 1, False, lambda: halo(reg_b, 3, 1, (-1, 1), True))
     reg_d[1] = x[2]
     halo(reg_d, 2, 1, (-1, 1), True)
 
     def scatter4(src, dst, index):
-        def body(k, c):
-            tg = (g + k) % NX
+        for tg in partners:
             remote(src.at[tg], dst.at[s], sems.at[0, index], sems.at[1, index], (tg, y)).start()
-            return c
-
-        lax.fori_loop(1, NX, body, 0)
 
     def pack_planes(field, out, own_slot):
         tmp[...] = field.T
@@ -584,7 +584,7 @@
         )
 
     def gas_advance(b, old, flow, store):
-        flux = reg_a[b + 1, pl.ds(257, 1), :]
+        flux = reg_x[b + 1, pl.ds(1, 1), :]
         for j in range(SEG):
             conc = old[b, rows(j), :]
             root = gas_g[b, rows(j), :]
@@ -651,6 +651,7 @@
         oxy_out[0, :, 128 * i : 128 * i + 128] = brick[i]
 
     halo(reg_a, 0, 2, (-1, 1, -2, 2), False)
+    halo(reg_x, 4, 2, (-1, 1, -2, 2), False)
     halo(reg_c, 1, 2, (-1, 1, -2, 2), False)
     halo(reg_d, 2, 1, (-1, 1), False)
     halo(reg_b, 3, 1, (-1, 1), False)
@@ -687,7 +688,8 @@
             buf(8 * NX, LANES),
             buf(2, LANES),
             buf(NX, 2, LANES),
-            buf(REGION, 264, LANES),
+            buf(REGION, 256, LANES),
+            buf(REGION, 8, LANES),
             buf(3, 256, LANES),
             buf(REGION, *block),
             buf(3, *block),
@@ -721,8 +723,8 @@
             pltpu.VMEM((1, LANES), jnp.int32),
             buf(1, LANES),
             pltpu.SemaphoreType.DMA((2, 6)),
-            pltpu.SemaphoreType.DMA((4, REGION)),
-            pltpu.SemaphoreType.DMA((4, REGION)),
+            pltpu.SemaphoreType.DMA((5, REGION)),
+            pltpu.SemaphoreType.DMA((5, REGION)),
             pltpu.SemaphoreType.DMA((6,)),
         ],
         compiler_params=pltpu.CompilerParams(

time: 58.8 us -> 54.9 us (0.934)
  Pallas kernels: 57.9 us -> 54.1 us
    pallas_call x1, Pallas kernels: 56.4 us -> 52.6 us  [local(): pl.pallas_call(kernel, out_shape=(jax.ShapeDtypeStruct((1, DEPTH, LANES),...]
where the time goes in v3:
time: 54.9 us; the launch traced here: 54.7 us
  Pallas kernels  54.1 us (99%)
  between operations  0.64 us (1%)
    pallas_call x1, Pallas kernels, local(): pl.pallas_call(kernel, out_shape=(jax.ShapeDtypeStruct((1, DEPTH, LANES),...  52.6 us
    pallas_call x1, Pallas kernels, local(): pl.pallas_call(finish, out_shape=tuple((jax.ShapeDtypeStruct(v.shape, f32...  1.53 us

profile of v3, /device:TPU:1, one launch (start us, length us, event | category | flops | bytes accessed | tf_op | source)
XLA Modules:
  0.0 54.7 jit_solution(18333441865513523875)
XLA Ops:
  0.6 52.6 %shard_map.77 = (f32[1,128,128]{2,1,0:T(8,128)}, f32[1,16,1024]{2,1,0:T(8,128)}) custom-call(f32[1,128,128]{2,1,0:T(8,128)} %head_ref.1, s32[1,128,128]{2,1,0:T(8,128)} %zone_ref.1, s32[1,128]{1,0:T(1,128)} %em_ref.1, f32[1,128,128]{2,1,0:T(8,128)} %oxy_ref.1, f32[1,128,128]{2,1,0:T(8,128)} %sul_ref.1, f32[1,128]{1,0:T(1,128)} %flux_ref.1), custom_call_target="tpu_custom_call" | custom-call | tf_op jit(solution)/shard_map/pallas_call | solution.py:674
  53.2 1.5 %shard_map.78 = (f32[1,128,128]{2,1,0:T(8,128)}, f32[1,16,1024]{2,1,0:T(8,128)}) custom-call(f32[1,128,128]{2,1,0:T(8,128)} %get-tuple-element.4.head, f32[1,16,1024]{2,1,0:T(8,128)} %get-tuple-element.5.oxygen), custom_call_target="tpu_custom_call" | custom-call | tf_op jit(solution)/shard_map/pallas_call | solution.py:734

commit v4 on v3

--- a/solution.py
+++ b/solution.py
@@ -97,7 +97,7 @@
     tmp, tmp2, send_a, recv_a, send_b, recv_b, send_x, recv_x, reg_a, reg_x, reg_b, reg_c, reg_d,
     cond, half_cap, se_old, raw, base, lat, face, row_a, row_c, fac, x, f,
     gas_g, gas_s, gas_f0, gas_f1, gas_c, gas_r,
-    send_h, recv_h, send_o, recv_o, brick, in_h, in_z, in_o, in_s, in_e, in_f,
+    send_h, recv_h, send_o, recv_o, in_h, in_z, in_o, in_s, in_e, in_f,
     sems, halo_s, halo_r, in_sem,
 ):
     g = lax.axis_index("gx")
@@ -626,29 +626,29 @@
     wait_all(recv_h.at[most4], sems.at[1, 3])
     field = planes(recv_h)
     for j in range(SEG):
-        head_out[0, pl.ds(j, SUB, stride=SEG), :] = field[8 * j : 8 * j + 8]
+        in_h[pl.ds(j, SUB, stride=SEG), :] = field[8 * j : 8 * j + 8]
+    result = pltpu.make_async_copy(in_h, head_out.at[0], in_sem.at[0])
+    result.start()
 
     wait_all(recv_o.at[most4], sems.at[1, 4])
     field = planes(recv_o)
     for j in range(SEG):
         tmp2[pl.ds(j, SUB, stride=SEG), :] = field[8 * j : 8 * j + 8]
 
-    def body_brick(k, c):
+    mine = pl.ds(pl.multiple_of(LANES * y, LANES), LANES)
+
+    def depths(b):
+        return tmp2.at[pl.ds(pl.multiple_of(16 * b, 16), 16)]
+
+    for k in (4, 5, 3, 6, 2, 7, 1):
         ty = (y + k) % NYD
-        remote(
-            tmp2.at[pl.ds(pl.multiple_of(16 * ty, 16), 16)],
-            brick.at[y],
-            sems.at[0, 5],
-            sems.at[1, 5],
-            (g, ty),
-        ).start()
-        return c
-
-    lax.fori_loop(1, NYD, body_brick, 0)
-    brick[y] = tmp2[pl.ds(pl.multiple_of(16 * y, 16), 16), :]
-    wait_all(brick.at[pl.ds(0, NYD - 1)], sems.at[1, 5])
-    for i in range(NYD):
-        oxy_out[0, :, 128 * i : 128 * i + 128] = brick[i]
+        remote(depths(ty), oxy_out.at[0, :, mine], sems.at[0, 5], sems.at[1, 5], (g, ty)).start()
+    kept = pltpu.make_async_copy(depths(y), oxy_out.at[0, :, mine], in_sem.at[1])
+    kept.start()
+    others = oxy_out.at[0, :, pl.ds(0, LANES * (NYD - 1))]
+    result.wait()
+    kept.wait()
+    wait_all(others, sems.at[1, 5])
 
     halo(reg_a, 0, 2, (-1, 1, -2, 2), False)
     halo(reg_x, 4, 2, (-1, 1, -2, 2), False)
@@ -660,7 +660,7 @@
     wait_all(recv_b.at[most8], sems.at[0, 2])
     wait_all(recv_h.at[most4], sems.at[0, 3])
     wait_all(recv_o.at[most4], sems.at[0, 4])
-    wait_all(brick.at[pl.ds(0, NYD - 1)], sems.at[0, 5])
+    wait_all(others, sems.at[0, 5])
 
 
 def local(pressure_head, material_zone, emitters, oxygen, sulfide_rate, air_flux):
@@ -678,7 +678,7 @@
             jax.ShapeDtypeStruct((1, DEPTH // NYD, LANES * NYD), f32),
         ),
         in_specs=[pl.BlockSpec(memory_space=pl.ANY)] * 6,
-        out_specs=(vmem, vmem),
+        out_specs=(pl.BlockSpec(memory_space=pl.ANY),) * 2,
         scratch_shapes=[
             buf(*block),
             buf(*block),
@@ -715,7 +715,6 @@
             buf(NX, COLS, LANES),
             buf(NX, COLS, LANES),
             buf(NX, COLS, LANES),
-            buf(NYD, DEPTH // NYD, LANES),
             buf(*block),
             pltpu.VMEM(block, jnp.int32),
             buf(*block),

time: 54.9 us -> 54.3 us (0.989)
  Pallas kernels: 54.1 us -> 53.4 us
    pallas_call x1, Pallas kernels: 52.6 us -> 51.9 us  [local(): pl.pallas_call(kernel, out_shape=(jax.ShapeDtypeStruct((1, DEPTH, LANES),...]
where the time goes in v4:
time: 54.3 us; the launch traced here: 54.1 us
  Pallas kernels  53.4 us (98%)
  between operations  0.64 us (1%)
    pallas_call x1, Pallas kernels, local(): pl.pallas_call(kernel, out_shape=(jax.ShapeDtypeStruct((1, DEPTH, LANES),...  51.9 us
    pallas_call x1, Pallas kernels, local(): pl.pallas_call(finish, out_shape=tuple((jax.ShapeDtypeStruct(v.shape, f32...  1.53 us

profile of v4, /device:TPU:1, one launch (start us, length us, event | category | flops | bytes accessed | tf_op | source)
XLA Modules:
  0.0 54.1 jit_solution(6406217034353878365)
XLA Ops:
  0.6 51.9 %shard_map.77 = (f32[1,128,128]{2,1,0:T(8,128)}, f32[1,16,1024]{2,1,0:T(8,128)}) custom-call(f32[1,128,128]{2,1,0:T(8,128)} %head_ref.1, s32[1,128,128]{2,1,0:T(8,128)} %zone_ref.1, s32[1,128]{1,0:T(1,128)} %em_ref.1, f32[1,128,128]{2,1,0:T(8,128)} %oxy_ref.1, f32[1,128,128]{2,1,0:T(8,128)} %sul_ref.1, f32[1,128]{1,0:T(1,128)} %flux_ref.1), custom_call_target="tpu_custom_call" | custom-call | tf_op jit(solution)/shard_map/pallas_call | solution.py:674
  52.6 1.5 %shard_map.78 = (f32[1,128,128]{2,1,0:T(8,128)}, f32[1,16,1024]{2,1,0:T(8,128)}) custom-call(f32[1,128,128]{2,1,0:T(8,128)} %get-tuple-element.4.head, f32[1,16,1024]{2,1,0:T(8,128)} %get-tuple-element.5.oxygen), custom_call_target="tpu_custom_call" | custom-call | tf_op jit(solution)/shard_map/pallas_call | solution.py:733

commit v5 on v4

--- a/solution.py
+++ b/solution.py
@@ -623,33 +623,6 @@
         return jnp.concatenate([src[i] for i in range(NX)], axis=0).T
 
     most4 = pl.ds(0, NX - 1)
-    wait_all(recv_h.at[most4], sems.at[1, 3])
-    field = planes(recv_h)
-    for j in range(SEG):
-        in_h[pl.ds(j, SUB, stride=SEG), :] = field[8 * j : 8 * j + 8]
-    result = pltpu.make_async_copy(in_h, head_out.at[0], in_sem.at[0])
-    result.start()
-
-    wait_all(recv_o.at[most4], sems.at[1, 4])
-    field = planes(recv_o)
-    for j in range(SEG):
-        tmp2[pl.ds(j, SUB, stride=SEG), :] = field[8 * j : 8 * j + 8]
-
-    mine = pl.ds(pl.multiple_of(LANES * y, LANES), LANES)
-
-    def depths(b):
-        return tmp2.at[pl.ds(pl.multiple_of(16 * b, 16), 16)]
-
-    for k in (4, 5, 3, 6, 2, 7, 1):
-        ty = (y + k) % NYD
-        remote(depths(ty), oxy_out.at[0, :, mine], sems.at[0, 5], sems.at[1, 5], (g, ty)).start()
-    kept = pltpu.make_async_copy(depths(y), oxy_out.at[0, :, mine], in_sem.at[1])
-    kept.start()
-    others = oxy_out.at[0, :, pl.ds(0, LANES * (NYD - 1))]
-    result.wait()
-    kept.wait()
-    wait_all(others, sems.at[1, 5])
-
     halo(reg_a, 0, 2, (-1, 1, -2, 2), False)
     halo(reg_x, 4, 2, (-1, 1, -2, 2), False)
     halo(reg_c, 1, 2, (-1, 1, -2, 2), False)
@@ -658,8 +631,35 @@
     wait_all(recv_a.at[most8], sems.at[0, 0])
     wait_all(recv_x.at[pl.ds(0, NX - 1)], sems.at[0, 1])
     wait_all(recv_b.at[most8], sems.at[0, 2])
+    wait_all(recv_h.at[most4], sems.at[1, 3])
+    field = planes(recv_h)
+    for j in range(SEG):
+        in_h[pl.ds(j, SUB, stride=SEG), :] = field[8 * j : 8 * j + 8]
+    result = pltpu.make_async_copy(in_h, head_out.at[0], in_sem.at[0])
+    result.start()
+
+    wait_all(recv_o.at[most4], sems.at[1, 4])
+    field = planes(recv_o)
+    for j in range(SEG):
+        tmp2[pl.ds(j, SUB, stride=SEG), :] = field[8 * j : 8 * j + 8]
+
+    mine = pl.ds(pl.multiple_of(LANES * y, LANES), LANES)
+
+    def depths(b):
+        return tmp2.at[pl.ds(pl.multiple_of(16 * b, 16), 16)]
+
+    for k in (4, 5, 3, 6, 2, 7, 1):
+        ty = (y + k) % NYD
+        remote(depths(ty), oxy_out.at[0, :, mine], sems.at[0, 5], sems.at[1, 5], (g, ty)).start()
+    kept = pltpu.make_async_copy(depths(y), oxy_out.at[0, :, mine], in_sem.at[1])
+    kept.start()
+    others = oxy_out.at[0, :, pl.ds(0, LANES * (NYD - 1))]
     wait_all(recv_h.at[most4], sems.at[0, 3])
     wait_all(recv_o.at[most4], sems.at[0, 4])
+    result.wait()
+    kept.wait()
+    wait_all(others, sems.at[1, 5])
+
     wait_all(others, sems.at[0, 5])
 
 

time: 54.3 us -> 54.2 us (level)
  no operation moved by 1% of the time
where the time goes in v5:
time: 54.2 us; the launch traced here: 54.1 us
  Pallas kernels  53.4 us (99%)
  between operations  0.64 us (1%)
    pallas_call x1, Pallas kernels, local(): pl.pallas_call(kernel, out_shape=(jax.ShapeDtypeStruct((1, DEPTH, LANES),...  51.9 us
    pallas_call x1, Pallas kernels, local(): pl.pallas_call(finish, out_shape=tuple((jax.ShapeDtypeStruct(v.shape, f32...  1.53 us

profile of v5, /device:TPU:1, one launch (start us, length us, event | category | flops | bytes accessed | tf_op | source)
XLA Modules:
  0.0 54.1 jit_solution(6910704631180450204)
XLA Ops:
  0.6 51.9 %shard_map.77 = (f32[1,128,128]{2,1,0:T(8,128)}, f32[1,16,1024]{2,1,0:T(8,128)}) custom-call(f32[1,128,128]{2,1,0:T(8,128)} %head_ref.1, s32[1,128,128]{2,1,0:T(8,128)} %zone_ref.1, s32[1,128]{1,0:T(1,128)} %em_ref.1, f32[1,128,128]{2,1,0:T(8,128)} %oxy_ref.1, f32[1,128,128]{2,1,0:T(8,128)} %sul_ref.1, f32[1,128]{1,0:T(1,128)} %flux_ref.1), custom_call_target="tpu_custom_call" | custom-call | tf_op jit(solution)/shard_map/pallas_call | solution.py:674
  52.5 1.5 %shard_map.78 = (f32[1,128,128]{2,1,0:T(8,128)}, f32[1,16,1024]{2,1,0:T(8,128)}) custom-call(f32[1,128,128]{2,1,0:T(8,128)} %get-tuple-element.4.head, f32[1,16,1024]{2,1,0:T(8,128)} %get-tuple-element.5.oxygen), custom_call_target="tpu_custom_call" | custom-call | tf_op jit(solution)/shard_map/pallas_call | solution.py:733

commit v6 on v5

--- a/solution.py
+++ b/solution.py
@@ -308,8 +308,6 @@
                     ) * (se - se_old[b, rows(j), :])
             return carry
 
-        lax.fori_loop(0, REGION, retain, 0)
-        meanwhile()
 
         def right_faces(b, carry):
             after = jnp.minimum(b + 1, REGION - 1)
@@ -322,7 +320,6 @@
                 face[b, rows(j), :] = mask * harmonic(k, near)
             return carry
 
-        lax.fori_loop(0, REGION, right_faces, 0)
 
         def assemble(b, carry):
             before = jnp.maximum(b - 1, 0)
@@ -352,7 +349,6 @@
                 row_c[b, rows(j), :] = los[j] * inv
             return carry
 
-        lax.fori_loop(0, REGION, assemble, 0)
 
         def factor(blocks):
             state = {}
@@ -435,8 +431,17 @@
                     put(b, LAST + k, value)
                     put(b, PREV + (k + 1) % 8, roll(value, 1, 0))
 
-        factor((0, 1, 2))
-        factor((3, 4))
+        lax.fori_loop(0, 3, retain, 0)
+        lax.fori_loop(1, 3, right_faces, 0)
+        assemble(2, 0)
+        factor((2,))
+        lax.fori_loop(3, REGION, retain, 0)
+        meanwhile()
+        right_faces(0, 0)
+        lax.fori_loop(3, REGION, right_faces, 0)
+        lax.fori_loop(0, 2, assemble, 0)
+        lax.fori_loop(3, REGION, assemble, 0)
+        factor((0, 1, 3, 4))
 
         def sources(b):
             before, after = max(b - 1, 0), min(b + 1, REGION - 1)

time: 54.2 us -> 53.8 us (level)
  no operation moved by 1% of the time
where the time goes in v6:
time: 53.8 us; the launch traced here: 53.6 us
  Pallas kernels  53 us (99%)
  between operations  0.64 us (1%)
    pallas_call x1, Pallas kernels, local(): pl.pallas_call(kernel, out_shape=(jax.ShapeDtypeStruct((1, DEPTH, LANES),...  51.5 us
    pallas_call x1, Pallas kernels, local(): pl.pallas_call(finish, out_shape=tuple((jax.ShapeDtypeStruct(v.shape, f32...  1.53 us

profile of v6, /device:TPU:1, one launch (start us, length us, event | category | flops | bytes accessed | tf_op | source)
XLA Modules:
  0.0 53.6 jit_solution(4197486651016579267)
XLA Ops:
  0.6 51.5 %shard_map.77 = (f32[1,128,128]{2,1,0:T(8,128)}, f32[1,16,1024]{2,1,0:T(8,128)}) custom-call(f32[1,128,128]{2,1,0:T(8,128)} %head_ref.1, s32[1,128,128]{2,1,0:T(8,128)} %zone_ref.1, s32[1,128]{1,0:T(1,128)} %em_ref.1, f32[1,128,128]{2,1,0:T(8,128)} %oxy_ref.1, f32[1,128,128]{2,1,0:T(8,128)} %sul_ref.1, f32[1,128]{1,0:T(1,128)} %flux_ref.1), custom_call_target="tpu_custom_call" | custom-call | tf_op jit(solution)/shard_map/pallas_call | solution.py:679
  52.1 1.5 %shard_map.78 = (f32[1,128,128]{2,1,0:T(8,128)}, f32[1,16,1024]{2,1,0:T(8,128)}) custom-call(f32[1,128,128]{2,1,0:T(8,128)} %get-tuple-element.4.head, f32[1,16,1024]{2,1,0:T(8,128)} %get-tuple-element.5.oxygen), custom_call_target="tpu_custom_call" | custom-call | tf_op jit(solution)/shard_map/pallas_call | solution.py:738
